TPU v7x, 256 devices: a whole 4x4x8 slice. The times are simulated.
256 devices in a mesh: frame: 16 (over z_hi, y), ref: 16 (over z_lo, x, core).
Axes of the slice: x: 4, y: 4, z: 8 (z_hi: 4, z_lo: 2; z = z_hi * 2 + z_lo), core: 2. Of those that a mesh axis runs over, the one named last changes fastest.
Arguments:
- latents: bfloat16 [16, 16, 256, 640], P('ref', 'frame'), may hold values from -6 to 6
- ref_hidden: bfloat16 [256, 640], P('ref'), may hold values from -6 to 6
- spatial_query: bfloat16 [640, 640], replicated, may hold values from -16 to 16
- spatial_key: bfloat16 [640, 640], replicated, may hold values from -1 to 1
- spatial_value: bfloat16 [640, 640], replicated, may hold values from -0.25 to 0.25
- spatial_out_w: bfloat16 [640, 640], replicated, may hold values from -0.25 to 0.25
- temporal_query: bfloat16 [640, 640], replicated, may hold values from -16 to 16
- temporal_key: bfloat16 [640, 640], replicated, may hold values from -1 to 1
- temporal_value: bfloat16 [640, 640], replicated, may hold values from -0.25 to 0.25
- temporal_out_w: bfloat16 [640, 640], replicated, may hold values from -0.25 to 0.25
Outputs:
- spatial_out: bfloat16 [16, 16, 256, 640], P('ref', 'frame')
- video_out: bfloat16 [16, 16, 256, 640], P('ref', 'frame')
All inputs are finite; a program needn't handle non-finite values.
Results may differ from a plain program's by a relative error of at most 0.014.
Values may be sent and summed in bfloat16 or wider, within the bound.
A program may use at most 64 MiB of HBM per device.

v0:
```python
import math

import jax
import jax.numpy as jnp
from jax import lax
from jax.sharding import PartitionSpec as P

HEADS = 8


epsilon = 1e-05


def layer_norm(values_in):
    values_in = values_in.astype(jnp.float32)
    center = values_in - jnp.mean(values_in, axis=-1, keepdims=True)
    spread = jnp.mean(center * center, axis=-1, keepdims=True)
    return center * lax.rsqrt(spread + epsilon)


def sinusoid(count, width):
    position = jnp.arange(count, dtype=jnp.float32)[:, None]
    index_pair = jnp.arange(width // 2, dtype=jnp.float32)[None, :]
    angle = position * jnp.exp(index_pair * (-2.0 * math.log(10000.0) / width))
    return jnp.stack([jnp.sin(angle), jnp.cos(angle)], axis=-1).reshape(count, width)


def softmax_rows(scores):
    shifted = jnp.exp(scores - jnp.max(scores, axis=-1, keepdims=True))
    return (shifted / jnp.sum(shifted, axis=-1, keepdims=True)).astype(jnp.bfloat16)


def project(rows, matrix):
    return jnp.dot(rows, matrix, preferred_element_type=jnp.float32).astype(jnp.bfloat16)


def attend_blocks(query_rows, key_rows, value_rows):
    row_count, width = query_rows.shape
    head_dim = width // HEADS
    scale = 1.0 / math.sqrt(head_dim)
    head_outputs = []
    for head_index in range(HEADS):
        lower = head_index * head_dim
        query_head = query_rows[:, lower : lower + head_dim]
        key_head = key_rows[:, lower : lower + head_dim]
        value_head = value_rows[:, lower : lower + head_dim]
        scores = (
            lax.dot_general(
                query_head, key_head, (((1,), (1,)), ((), ())), preferred_element_type=jnp.float32
            )
            * scale
        )
        weights = softmax_rows(scores)
        head_outputs.append(jnp.dot(weights, value_head, preferred_element_type=jnp.float32))
    block_outputs = [jnp.concatenate(head_outputs, axis=1).astype(jnp.bfloat16)]
    return jnp.concatenate(block_outputs, axis=0)


def body(
    latents,
    ref_hidden,
    spatial_query,
    spatial_key,
    spatial_value,
    spatial_out_w,
    temporal_query,
    temporal_key,
    temporal_value,
    temporal_out_w,
):
    frames_here = latents.shape[1]
    grid_tokens = latents.shape[2]
    width = latents.shape[3]
    head_dim = width // HEADS
    ref_normed = layer_norm(ref_hidden).astype(jnp.bfloat16)
    local_keys = project(ref_normed, spatial_key)
    local_values = project(ref_normed, spatial_value)
    ref_key_rows, ref_value_rows = (
        lax.all_gather(local_keys, "ref", axis=0, tiled=True),
        lax.all_gather(local_values, "ref", axis=0, tiled=True),
    )
    video = latents[0]
    normed = layer_norm(video).astype(jnp.bfloat16).reshape(frames_here * grid_tokens, width)
    query_rows = project(normed, spatial_query).reshape(frames_here, grid_tokens, width)
    key_rows = project(normed, spatial_key).reshape(frames_here, grid_tokens, width)
    value_rows = project(normed, spatial_value).reshape(frames_here, grid_tokens, width)

    def frame_attention(packed):
        frame_queries, frame_keys, frame_values = packed
        key_list = jnp.concatenate([frame_keys, ref_key_rows], axis=0)
        value_list = jnp.concatenate([frame_values, ref_value_rows], axis=0)
        return attend_blocks(frame_queries, key_list, value_list)

    attended = lax.map(frame_attention, (query_rows, key_rows, value_rows))
    update = jnp.dot(
        attended.reshape(frames_here * grid_tokens, width),
        spatial_out_w,
        preferred_element_type=jnp.float32,
    ).reshape(frames_here, grid_tokens, width)
    spatial_result = (video.astype(jnp.float32) + update).astype(jnp.bfloat16)
    groups = lax.axis_size("frame")
    spread_rows = spatial_result.reshape(frames_here, groups, grid_tokens // groups, width)
    piece = lax.all_to_all(spread_rows, "frame", split_axis=1, concat_axis=0, tiled=True)
    clip_len = piece.shape[0]
    count = piece.shape[2]
    clip_rows = piece.reshape(clip_len, count, width)
    time_norm = (layer_norm(clip_rows) + sinusoid(clip_len, width)[:, None, :]).astype(jnp.bfloat16)
    flat = time_norm.reshape(clip_len * count, width)
    query_heads = project(flat, temporal_query).reshape(clip_len, count, HEADS, head_dim)
    key_heads = project(flat, temporal_key).reshape(clip_len, count, HEADS, head_dim)
    value_heads = project(flat, temporal_value).reshape(clip_len, count, HEADS, head_dim)
    scores = jnp.einsum(
        "fthd,ethd->thfe", query_heads, key_heads, preferred_element_type=jnp.float32
    ) * (1.0 / math.sqrt(head_dim))
    weights = softmax_rows(scores)
    mixed = jnp.einsum("thfe,ethd->fthd", weights, value_heads, preferred_element_type=jnp.float32)
    mixed = mixed.reshape(clip_len * count, width).astype(jnp.bfloat16)
    time_update = jnp.dot(mixed, temporal_out_w, preferred_element_type=jnp.float32)
    result = (clip_rows.astype(jnp.float32) + time_update.reshape(clip_len, count, width)).astype(
        jnp.bfloat16
    )
    merged = lax.all_to_all(
        result.reshape(clip_len, 1, count, width), "frame", split_axis=0, concat_axis=1, tiled=True
    )
    video_result = merged.reshape(frames_here, grid_tokens, width)
    return (spatial_result[None], video_result[None])


def solution(mesh):
    return jax.shard_map(
        body,
        mesh=mesh,
        in_specs=(
            P("ref", "frame", None, None),
            P("ref", None),
            P(),
            P(),
            P(),
            P(),
            P(),
            P(),
            P(),
            P(),
        ),
        out_specs=(P("ref", "frame", None, None), P("ref", "frame", None, None)),
        check_vma=False,
    )
```

profile of v0, /device:TPU:2, one launch (start us, length us, event | category | flops | bytes accessed | tf_op | source)
XLA Modules:
  0.0 108.3 jit_solution(2050266346444587427)
XLA Ops:
  0.7 1.2 %convert_reduce_fusion = f32[256]{0:T(256)S(1)} fusion(bf16[1,1,256,640]{3,2,1,0:T(8,128)(2,1)} %param.10), kind=kLoop, calls=%fused_computation.73 | loop fusion | flops 327424 | bytes 328704 | tf_op jit(solution)/shard_map/reduce_sum | solution.py:16
  2.1 0.5 copy-done.10
  2.9 0.5 convolution_convert_fusion.5
  3.5 0.3 convolution_convert_fusion.16
  3.8 0.9 copy-done.4
  4.6 0.5 convolution_convert_fusion.4
  5.2 0.3 convolution_convert_fusion.15
  5.4 0.9 copy-done.11
  6.3 0.5 convolution_convert_fusion.6
  6.8 19.1 %all_gather.6 = bf16[256,640]{1,0:T(8,128)(2,1)S(1)} all-gather(bf16[16,640]{1,0:T(8,128)(2,1)S(1)} %convolution_convert_fusion.16), channel_id=1, replica_groups=mesh['frame'=16,'ref'=16] {'ref'}, dimensions={0}, use_global_device_ids=true | all-gather | bytes 348160 | tf_op jit(solution)/shard_map/all_gather | solution.py:79
  25.9 0.3 fusion.113
  26.2 0.4 fusion.114
  26.6 0.4 fusion.115
  27.0 0.4 fusion.116
  27.4 0.4 fusion.117
  27.8 0.4 fusion.118
  28.2 0.4 fusion.119
  28.6 0.4 fusion.120
  29.0 19.2 %all_gather.7 = bf16[256,640]{1,0:T(8,128)(2,1)S(1)} all-gather(bf16[16,640]{1,0:T(8,128)(2,1)S(1)} %convolution_convert_fusion.15), channel_id=1, replica_groups=mesh['frame'=16,'ref'=16] {'ref'}, dimensions={0}, use_global_device_ids=true | all-gather | bytes 348160 | tf_op jit(solution)/shard_map/all_gather | solution.py:80
  48.6 0.3 fusion.14
  48.9 0.4 fusion.13
  49.3 0.2 fusion.32
  49.5 0.4 fusion.12
  49.8 0.2 fusion.33
  50.1 0.4 fusion.11
  50.4 0.2 fusion.34
  50.7 0.4 fusion.10
  51.2 0.4 fusion.9
  51.8 0.4 fusion.8
  52.2 0.2 fusion.37
  52.4 0.3 fusion.7
  52.8 0.8 copy-done.2
  53.6 1.2 %fusion.4 = bf16[256,640]{1,0:T(8,128)(2,1)} fusion(bf16[256,640]{0,1:T(8,128)(2,1)S(1)} %fusion.7, bf16[640,640]{1,0:T(8,128)(2,1)S(1)} %copy-done.2, bf16[1,1,256,640]{3,2,1,0:T(8,128)(2,1)S(1)} %copy-done.1), kind=kOutput, calls=%fused_computation.16 | convolution fusion | flops 210206720 | bytes 1802240 | tf_op jit(solution)/shard_map/dot_general | solution.py:95
  54.8 10.3 %all-to-all-start = ((bf16[1,16,16,640]{3,2,0,1:T(8,128)(2,1)}), bf16[1,16,16,640]{3,2,0,1:T(8,128)(2,1)S(1)}, u32[]{:S(2)}, u32[]{:S(2)}) async-start(bf16[1,16,16,640]{3,2,0,1:T(8,128)(2,1)} %bitcast.4), calls=%async_computation | async-start | bytes 655360 | tf_op jit(solution)/shard_map/all_to_all | solution.py:103
  65.5 13.9 %all-to-all-done = bf16[1,16,16,640]{3,2,0,1:T(8,128)(2,1)S(1)} async-done(((bf16[1,16,16,640]{3,2,0,1:T(8,128)(2,1)}), bf16[1,16,16,640]{3,2,0,1:T(8,128)(2,1)S(1)}, u32[]{:S(2)}, u32[]{:S(2)}) %all-to-all-start) | async-done | bytes 327712 | tf_op jit(solution)/shard_map/all_to_all | solution.py:103
  80.2 0.5 convolution_convert_fusion.2
  80.7 1.4 %reshape.272 = bf16[16,16,8,80]{3,2,1,0:T(8,128)(2,1)} reshape(bf16[256,640]{1,0:T(8,128)(2,1)S(1)} %convolution_convert_fusion.2) | data formatting | bytes 655360 | tf_op jit(solution)/shard_map/reshape | solution.py:109
  82.0 0.5 convolution_convert_fusion.1
  82.5 0.6 reshape.273
  83.2 0.5 convolution_convert_fusion.3
  83.7 1.4 %reshape.271 = bf16[16,16,8,80]{3,2,1,0:T(8,128)(2,1)} reshape(bf16[256,640]{1,0:T(8,128)(2,1)S(1)} %convolution_convert_fusion.3) | data formatting | bytes 655360 | tf_op jit(solution)/shard_map/reshape | solution.py:111
  85.1 2.0 %fusion.121 = (f32[16,8,16]{2,1,0:T(8,128)S(1)}, f32[16,8,16,16]{2,3,1,0:T(8,128)}) fusion(bf16[16,16,8,80]{3,2,1,0:T(8,128)(2,1)S(1)} %reshape.273, bf16[16,16,8,80]{3,2,1,0:T(8,128)(2,1)S(1)} %copy-done.8), kind=kOutput, calls=%fused_computation.187 | convolution fusion | flops 5341199 | bytes 794624 | tf_op jit(solution)/shard_map/sub | solution.py:29
  87.1 1.7 %fusion.3 = bf16[16,16,8,80]{3,0,2,1:T(8,128)(2,1)S(1)} fusion(f32[16,8,16,16]{2,3,1,0:T(8,128)} %get-tuple-element.42, bf16[16,16,8,80]{3,2,1,0:T(8,128)(2,1)S(1)} %copy-done.9, f32[16,8,16]{2,1,0:T(8,128)S(1)} %get-tuple-element.41), kind=kOutput, calls=%fused_computation.15 | convolution fusion | flops 5472256 | bytes 794624 | tf_op jit(solution)/shard_map/thfe,ethd->fthd/dot_general | solution.py:116
  88.9 0.4 convert_element_type.166
  89.3 0.6 copy-done.3
  89.9 0.5 fusion.6
  90.4 17.2 %all_to_all.8 = bf16[16,1,16,640]{3,2,1,0:T(8,128)(2,1)S(1)} all-to-all(bf16[16,1,16,640]{3,2,1,0:T(8,128)(2,1)S(1)} %fusion.6), channel_id=1, replica_groups=mesh['frame'=16,'ref'=16] {'frame'}, dimensions={0} | all-to-all | bytes 655360 | tf_op jit(solution)/shard_map/all_to_all | solution.py:122
  107.5 0.7 copy.59
  (43 shorter events, 2.9 us)
Async XLA Ops:
  0.6 2.3 %copy-start = (bf16[640,640]{1,0:T(8,128)(2,1)S(1)}, bf16[640,640]{1,0:T(8,128)(2,1)}, u32[]{:S(2)}) copy-start(bf16[640,640]{1,0:T(8,128)(2,1)} %param.13) | copy-start | bytes 2457604
  0.6 1.2 %copy-start.1 = (bf16[1,1,256,640]{3,2,1,0:T(8,128)(2,1)S(1)}, bf16[1,1,256,640]{3,2,1,0:T(8,128)(2,1)}, u32[]{:S(2)}) copy-start(bf16[1,1,256,640]{3,2,1,0:T(8,128)(2,1)} %param.10) | copy-start | bytes 983044
  1.9 0.7 copy-start.10
  3.5 1.1 %copy-start.4 = (bf16[640,640]{1,0:T(8,128)(2,1)S(1)}, bf16[640,640]{1,0:T(8,128)(2,1)}, u32[]{:S(2)}) copy-start(bf16[640,640]{1,0:T(8,128)(2,1)} %param.14) | copy-start | bytes 2457604
  5.1 1.1 %copy-start.11 = (bf16[640,640]{1,0:T(8,128)(2,1)S(1)}, bf16[640,640]{1,0:T(8,128)(2,1)}, u32[]{:S(2)}) copy-start(bf16[640,640]{1,0:T(8,128)(2,1)} %param.12) | copy-start | bytes 2457604
  52.4 1.2 %copy-start.2 = (bf16[640,640]{1,0:T(8,128)(2,1)S(1)}, bf16[640,640]{1,0:T(8,128)(2,1)}, u32[]{:S(2)}) copy-start(bf16[640,640]{1,0:T(8,128)(2,1)} %param.15) | copy-start | bytes 2457604
  54.8 24.7 %all-to-all-start = ((bf16[1,16,16,640]{3,2,0,1:T(8,128)(2,1)}), bf16[1,16,16,640]{3,2,0,1:T(8,128)(2,1)S(1)}, u32[]{:S(2)}, u32[]{:S(2)}) async-start(bf16[1,16,16,640]{3,2,0,1:T(8,128)(2,1)} %bitcast.4), calls=%async_computation | async-start | bytes 655360 | tf_op jit(solution)/shard_map/all_to_all | solution.py:103
  65.4 14.8 %copy-start.5 = (bf16[640,640]{1,0:T(8,128)(2,1)S(1)}, bf16[640,640]{1,0:T(8,128)(2,1)}, u32[]{:S(2)}) copy-start(bf16[640,640]{1,0:T(8,128)(2,1)} %param.16) | copy-start | bytes 2457604
  80.2 1.8 %copy-start.6 = (bf16[640,640]{1,0:T(8,128)(2,1)S(1)}, bf16[640,640]{1,0:T(8,128)(2,1)}, u32[]{:S(2)}) copy-start(bf16[640,640]{1,0:T(8,128)(2,1)} %param.17) | copy-start | bytes 2457604
  82.0 1.1 %copy-start.7 = (bf16[640,640]{1,0:T(8,128)(2,1)S(1)}, bf16[640,640]{1,0:T(8,128)(2,1)}, u32[]{:S(2)}) copy-start(bf16[640,640]{1,0:T(8,128)(2,1)} %param.18) | copy-start | bytes 2457604
  83.7 1.4 %copy-start.8 = (bf16[16,16,8,80]{3,2,1,0:T(8,128)(2,1)S(1)}, bf16[16,16,8,80]{3,2,1,0:T(8,128)(2,1)}, u32[]{:S(2)}) copy-start(bf16[16,16,8,80]{3,2,1,0:T(8,128)(2,1)} %reshape.272) | copy-start | bytes 983044
  85.1 2.0 %copy-start.9 = (bf16[16,16,8,80]{3,2,1,0:T(8,128)(2,1)S(1)}, bf16[16,16,8,80]{3,2,1,0:T(8,128)(2,1)}, u32[]{:S(2)}) copy-start(bf16[16,16,8,80]{3,2,1,0:T(8,128)(2,1)} %reshape.271) | copy-start | bytes 983044
  88.8 1.2 %copy-start.3 = (bf16[640,640]{1,0:T(8,128)(2,1)S(1)}, bf16[640,640]{1,0:T(8,128)(2,1)}, u32[]{:S(2)}) copy-start(bf16[640,640]{1,0:T(8,128)(2,1)} %param.19) | copy-start | bytes 2457604
where the time goes:
time: 109 us; the launch traced here: 108 us
  blocking collectives  55.4 us (51%)
  matrix products  14.7 us (13%)
  waiting for transfers between devices  13.9 us (13%)
  starting transfers between devices  10.3 us (9%)
  local copies, waits for them, and re-layouts  8.81 us (8%)
  other arithmetic  4.22 us (4%)
    all_gather x1, blocking collectives, body(): lax.all_gather(local_values, 'ref', axis=0, tiled=True)  19.2 us
    all_gather x1, blocking collectives, body(): lax.all_gather(local_keys, 'ref', axis=0, tiled=True)  19.1 us
    all_to_all x1, blocking collectives, body(): lax.all_to_all(result.reshape(clip_len, 1, count, width), 'frame', split_...  17.2 us
    all_to_all x1, waiting for transfers between devices, body(): lax.all_to_all(spread_rows, 'frame', split_axis=1, concat_axis=0, tiled=T...  13.9 us
    all_to_all x1, starting transfers between devices, body(): lax.all_to_all(spread_rows, 'frame', split_axis=1, concat_axis=0, tiled=T...  10.3 us
    unnamed x25, local copies, waits for them, and re-layouts  4.5 us
    dot_general x8, matrix products, project(): jnp.dot(rows, matrix, preferred_element_type=jnp.float32)  3.47 us
    dot_general x8, matrix products, attend_blocks(): lax.dot_general(query_head, key_head, (((1,), (1,)), ((), ())), preferred...  3.08 us
  transfers between devices with their start and end apart: 1, of which 1 were waited for; matrix products, arithmetic and copies ran while one was open for 0% of the time, Pallas kernels for 0%

commit v1 on v0

v1 whole, which is shorter than its diff:
```python
import functools
import math

import jax
import jax.numpy as jnp
import numpy as np
from jax import lax
from jax.experimental import pallas as pl
from jax.experimental.pallas import tpu as pltpu
from jax.sharding import PartitionSpec as P

MESH = pl.DeviceIdType.MESH
HEADS = 8
DIM = 80
WIDTH = 640
TOKENS = 256
FRAMES = 16
PIECES = 16
CHUNKS = 2
ROWS = TOKENS // CHUNKS
EACH = ROWS // FRAMES
EPSILON = 1e-05
SCALE = 1.0 / math.sqrt(DIM)
FACTOR = SCALE * math.log2(math.e)

FRAME_PEERS = sorted(
    [(a, b) for a in range(4) for b in range(4) if a or b],
    key=lambda o: -(2 * min(o[0], 4 - o[0]) + min(o[1], 4 - o[1])),
)
REF_PEERS = sorted(
    [(a, b, c) for a in range(2) for b in range(4) for c in range(2) if a or b or c],
    key=lambda o: -(2 * o[0] + 2 * min(o[1], 4 - o[1]) + o[2]),
)


def sinusoid(count, width):
    position = np.arange(count, dtype=np.float64)[:, None]
    pair = np.arange(width // 2, dtype=np.float64)[None, :]
    angle = position * np.exp(pair * (-2.0 * math.log(10000.0) / width))
    return np.stack([np.sin(angle), np.cos(angle)], axis=-1).reshape(count, width).astype(np.float32)


def layer_norm(rows):
    center = rows - jnp.mean(rows, axis=-1, keepdims=True)
    spread = jnp.mean(center * center, axis=-1, keepdims=True)
    return center * lax.rsqrt(spread + EPSILON)


def slab(head):
    low = head * DIM
    start = low // 128 * 128
    stop = -(-(low + DIM) // 128) * 128
    return start, stop - start, low - start


def head_lanes(head):
    start, wide, offset = slab(head)
    lane = lax.broadcasted_iota(jnp.int32, (1, wide), 1)
    return lane, (lane >= offset) & (lane < offset + DIM)


def ones_lane(head):
    start, wide, offset = slab(head)
    return 0 if offset > 0 else wide - 1


def masked_queries(rows, head):
    start, wide, _ = slab(head)
    _, inside = head_lanes(head)
    return jnp.where(inside, rows[:, start : start + wide], 0.0).astype(jnp.bfloat16)


def padded_values(rows, head):
    start, wide, _ = slab(head)
    lane, inside = head_lanes(head)
    filler = jnp.where(lane == ones_lane(head), 1.0, 0.0)
    return jnp.where(inside, rows[:, start : start + wide], filler).astype(jnp.bfloat16)


def attend(queries, keys_of, values_of, allowed=None):
    tiles = {}
    for head in range(HEADS):
        start, wide, offset = slab(head)
        scores = lax.dot_general(
            masked_queries(queries, head), keys_of(start, wide), (((1,), (1,)), ((), ())), preferred_element_type=jnp.float32
        )
        if allowed is not None:
            scores = jnp.where(allowed, scores, -1e30)
        top = jnp.max(scores, axis=-1, keepdims=True)
        weights = jnp.exp2((scores - top) * FACTOR).astype(jnp.bfloat16)
        mixed = jnp.dot(weights, values_of(head), preferred_element_type=jnp.float32)
        at = ones_lane(head)
        mixed = mixed * (1.0 / mixed[:, at : at + 1])
        lane, inside = head_lanes(head)
        for j in range(wide // 128):
            tile, cut = start // 128 + j, slice(j * 128, (j + 1) * 128)
            if tile in tiles:
                tiles[tile] = jnp.where(inside[:, cut], mixed[:, cut], tiles[tile])
            else:
                tiles[tile] = mixed[:, cut]
    return jnp.concatenate([tiles[t] for t in range(WIDTH // 128)], axis=1)


def project(rows, matrix):
    return jnp.dot(rows, matrix, preferred_element_type=jnp.float32)


def kernel(
    lat_hbm, ref_hbm, wq, wk, wv, wo, tq, tk, tv, to, pe_hbm,
    out_s, out_v,
    lat, ref_raw, ref_all, w, pe, queries, keys, values, own, got, back,
    load_sem, ref_send, ref_recv, go_send, go_recv, back_send, back_recv, out_sem,
):
    mine_f, mine_r = lax.axis_index("frame"), lax.axis_index("ref")
    zh, y = mine_f // 4, mine_f % 4
    zl, x, core = mine_r // 8, (mine_r // 2) % 4, mine_r % 2

    def frame_at(offset):
        return ((zh + offset[0]) % 4) * 4 + (y + offset[1]) % 4

    def ref_at(offset):
        return (((zl + offset[0]) % 2) * 4 + (x + offset[1]) % 4) * 2 + (core + offset[2]) % 2

    loads = [
        pltpu.make_async_copy(ref_hbm, ref_raw, load_sem.at[0]),
        pltpu.make_async_copy(lat_hbm, lat, load_sem.at[1]),
        pltpu.make_async_copy(pe_hbm, pe, load_sem.at[2]),
    ]
    weights = [
        pltpu.make_async_copy(matrix, w.at[i], load_sem.at[3 + i])
        for i, matrix in enumerate((wq, wk, wv, wo, tq, tk, tv, to))
    ]
    loads[0].start()
    loads[1].start()
    for copy in weights:
        copy.start()
    loads[2].start()

    barrier = pltpu.get_barrier_semaphore()
    for offset in FRAME_PEERS:
        pl.semaphore_signal(barrier, inc=1, device_id=(frame_at(offset), mine_r), device_id_type=MESH)
    for offset in REF_PEERS:
        pl.semaphore_signal(barrier, inc=1, device_id=(mine_f, ref_at(offset)), device_id_type=MESH)

    loads[0].wait()
    slot = pl.ds(pl.multiple_of(mine_r * PIECES, PIECES), PIECES)
    ref_all[slot, :] = layer_norm(ref_raw[...].astype(jnp.float32)).astype(jnp.bfloat16)
    pl.semaphore_wait(barrier, len(FRAME_PEERS) + len(REF_PEERS))
    ref_copies = []
    for k, offset in enumerate(REF_PEERS):
        copy = pltpu.make_async_remote_copy(
            src_ref=ref_all.at[slot, :], dst_ref=ref_all.at[slot, :],
            send_sem=ref_send.at[k], recv_sem=ref_recv.at[mine_r],
            device_id=(mine_f, ref_at(offset)), device_id_type=MESH,
        )
        copy.start()
        ref_copies.append(copy)

    loads[1].wait()
    normed = layer_norm(lat[...].astype(jnp.float32)).astype(jnp.bfloat16)
    weights[0].wait()
    queries[...] = project(normed, w[0]).astype(jnp.bfloat16)
    weights[1].wait()
    keys[0:TOKENS, :] = project(normed, w[1]).astype(jnp.bfloat16)
    weights[2].wait()
    own_values = project(normed, w[2]).astype(jnp.bfloat16)
    for head in range(HEADS):
        wide = slab(head)[1]
        values[head, 0:TOKENS, 0:wide] = padded_values(own_values, head)

    for k, offset in enumerate(REF_PEERS):
        source = ref_at(offset)
        there = pl.ds(pl.multiple_of(source * PIECES, PIECES), PIECES)
        pltpu.make_async_remote_copy(
            src_ref=ref_all.at[there, :], dst_ref=ref_all.at[there, :],
            send_sem=ref_send.at[k], recv_sem=ref_recv.at[source],
            device_id=(mine_f, source), device_id_type=MESH,
        ).wait_recv()
    reference = ref_all[...]
    keys[TOKENS : 2 * TOKENS, :] = project(reference, w[1]).astype(jnp.bfloat16)
    ref_values = project(reference, w[2]).astype(jnp.bfloat16)
    for head in range(HEADS):
        wide = slab(head)[1]
        values[head, TOKENS : 2 * TOKENS, 0:wide] = padded_values(ref_values, head)
    weights[3].wait()

    go_copies, out_copies = [], []
    for chunk in range(CHUNKS):
        rows = slice(chunk * ROWS, (chunk + 1) * ROWS)
        attended = attend(
            queries[rows, :],
            lambda start, wide: keys[:, start : start + wide],
            lambda head: values[head, :, 0 : slab(head)[1]],
        ).astype(jnp.bfloat16)
        result = lat[rows, :].astype(jnp.float32) + project(attended, w[3])
        own[chunk] = result.reshape(FRAMES, EACH, WIDTH).astype(jnp.bfloat16)
        for k, offset in enumerate(FRAME_PEERS):
            target = frame_at(offset)
            copy = pltpu.make_async_remote_copy(
                src_ref=own.at[chunk, target], dst_ref=got.at[chunk, mine_f],
                send_sem=go_send.at[chunk, k], recv_sem=go_recv.at[chunk, mine_f],
                device_id=(target, mine_r), device_id_type=MESH,
            )
            copy.start()
            go_copies.append(copy)
        got[chunk, pl.ds(mine_f, 1)] = own[chunk, pl.ds(mine_f, 1)]
        copy = pltpu.make_async_copy(
            own.at[chunk], out_s.at[pl.ds(chunk * FRAMES, FRAMES)], out_sem.at[chunk]
        )
        copy.start()
        out_copies.append(copy)

    loads[2].wait()
    for copy in weights[4:]:
        copy.wait()
    row = lax.broadcasted_iota(jnp.int32, (ROWS, ROWS), 0)
    column = lax.broadcasted_iota(jnp.int32, (ROWS, ROWS), 1)
    allowed = row % EACH == column % EACH
    back_copies = []
    for chunk in range(CHUNKS):
        for k, offset in enumerate(FRAME_PEERS):
            source = frame_at(offset)
            pltpu.make_async_remote_copy(
                src_ref=own.at[chunk, source], dst_ref=got.at[chunk, source],
                send_sem=go_send.at[chunk, k], recv_sem=go_recv.at[chunk, source],
                device_id=(source, mine_r), device_id_type=MESH,
            ).wait_recv()
        clip = got[chunk].astype(jnp.float32).reshape(ROWS, WIDTH)
        normed = (layer_norm(clip) + pe[...]).astype(jnp.bfloat16)
        time_queries = project(normed, w[4]).astype(jnp.bfloat16)
        time_keys = project(normed, w[5]).astype(jnp.bfloat16)
        time_values = project(normed, w[6]).astype(jnp.bfloat16)
        attended = attend(
            time_queries,
            lambda start, wide: time_keys[:, start : start + wide],
            lambda head: padded_values(time_values, head),
            allowed,
        ).astype(jnp.bfloat16)
        result = clip + project(attended, w[7])
        back[chunk] = result.reshape(FRAMES, EACH, WIDTH).astype(jnp.bfloat16)
        for k, offset in enumerate(FRAME_PEERS):
            target = frame_at(offset)
            copy = pltpu.make_async_remote_copy(
                src_ref=back.at[chunk, target], dst_ref=out_v.at[chunk * FRAMES + mine_f],
                send_sem=back_send.at[chunk, k], recv_sem=back_recv.at[chunk, mine_f],
                device_id=(target, mine_r), device_id_type=MESH,
            )
            copy.start()
            back_copies.append(copy)
        copy = pltpu.make_async_copy(
            back.at[chunk, mine_f], out_v.at[chunk * FRAMES + mine_f], out_sem.at[CHUNKS + chunk]
        )
        copy.start()
        out_copies.append(copy)

    for chunk in range(CHUNKS):
        for k, offset in enumerate(FRAME_PEERS):
            source = frame_at(offset)
            pltpu.make_async_remote_copy(
                src_ref=back.at[chunk, source], dst_ref=out_v.at[chunk * FRAMES + source],
                send_sem=back_send.at[chunk, k], recv_sem=back_recv.at[chunk, source],
                device_id=(source, mine_r), device_id_type=MESH,
            ).wait_recv()
    for copy in ref_copies + go_copies + back_copies:
        copy.wait_send()
    for copy in out_copies:
        copy.wait()


def body(latents, ref_hidden, *matrices):
    any_space = pl.BlockSpec(memory_space=pl.ANY)
    pe = jnp.asarray(np.repeat(sinusoid(FRAMES, WIDTH), EACH, axis=0))
    shape = jax.ShapeDtypeStruct((CHUNKS * FRAMES, EACH, WIDTH), jnp.bfloat16)
    spatial, video = pl.pallas_call(
        kernel,
        out_shape=(shape, shape),
        in_specs=[any_space] * 11,
        out_specs=(any_space, any_space),
        scratch_shapes=[
            pltpu.VMEM((TOKENS, WIDTH), jnp.bfloat16),
            pltpu.VMEM((PIECES, WIDTH), jnp.bfloat16),
            pltpu.VMEM((TOKENS, WIDTH), jnp.bfloat16),
            pltpu.VMEM((8, WIDTH, WIDTH), jnp.bfloat16),
            pltpu.VMEM((ROWS, WIDTH), jnp.float32),
            pltpu.VMEM((TOKENS, WIDTH), jnp.bfloat16),
            pltpu.VMEM((2 * TOKENS, WIDTH), jnp.bfloat16),
            pltpu.VMEM((HEADS, 2 * TOKENS, 256), jnp.bfloat16),
            pltpu.VMEM((CHUNKS, FRAMES, EACH, WIDTH), jnp.bfloat16),
            pltpu.VMEM((CHUNKS, FRAMES, EACH, WIDTH), jnp.bfloat16),
            pltpu.VMEM((CHUNKS, FRAMES, EACH, WIDTH), jnp.bfloat16),
            pltpu.SemaphoreType.DMA((11,)),
            pltpu.SemaphoreType.DMA((16,)),
            pltpu.SemaphoreType.DMA((16,)),
            pltpu.SemaphoreType.DMA((CHUNKS, 16)),
            pltpu.SemaphoreType.DMA((CHUNKS, 16)),
            pltpu.SemaphoreType.DMA((CHUNKS, 16)),
            pltpu.SemaphoreType.DMA((CHUNKS, 16)),
            pltpu.SemaphoreType.DMA((2 * CHUNKS,)),
        ],
        compiler_params=pltpu.CompilerParams(
            collective_id=0, has_side_effects=True, vmem_limit_bytes=48 * 2**20
        ),
        cost_estimate=pl.CostEstimate(flops=3_500_000_000, bytes_accessed=8_000_000, transcendentals=1_500_000),
    )(latents.reshape(TOKENS, WIDTH), ref_hidden, *matrices, pe)
    whole = (1, 1, TOKENS, WIDTH)
    return spatial.reshape(whole), video.reshape(whole)


def solution(mesh):
    split = P("ref", "frame", None, None)
    return jax.shard_map(
        body,
        mesh=mesh,
        in_specs=(split, P("ref", None)) + (P(),) * 8,
        out_specs=(split, split),
        check_vma=False,
    )
```

time: 109 us -> 51.6 us (0.47)
  the two profiles are of different devices: /device:TPU:2 before, /device:TPU:1 now
where the time goes in v1:
time: 51.6 us; the launch traced here: 51.1 us
  Pallas kernels  40.6 us (79%)
  local copies, waits for them, and re-layouts  9.84 us (19%)
  between operations  0.66 us (1%)
    pallas_call x1, Pallas kernels, body(): pl.pallas_call(kernel, out_shape=(shape, shape), in_specs=[any_space] * 1...  40.6 us
    unnamed x18, local copies, waits for them, and re-layouts  9.84 us

profile of v1, /device:TPU:1, one launch (start us, length us, event | category | flops | bytes accessed | tf_op | source)
XLA Modules:
  0.0 51.1 jit_solution(9343702606164472722)
XLA Ops:
  0.6 0.0 copy-start
  0.6 1.1 %copy-done = bf16[640,640]{1,0:T(8,128)(2,1)S(1)} copy-done((bf16[640,640]{1,0:T(8,128)(2,1)S(1)}, bf16[640,640]{1,0:T(8,128)(2,1)}, u32[]{:S(2)}) %copy-start) | copy-done | bytes 819224
  1.8 0.0 copy-start.1
  1.8 1.1 %copy-done.1 = bf16[640,640]{1,0:T(8,128)(2,1)S(1)} copy-done((bf16[640,640]{1,0:T(8,128)(2,1)S(1)}, bf16[640,640]{1,0:T(8,128)(2,1)}, u32[]{:S(2)}) %copy-start.1) | copy-done | bytes 819224
  2.9 0.0 copy-start.2
  2.9 1.1 %copy-done.2 = bf16[640,640]{1,0:T(8,128)(2,1)S(1)} copy-done((bf16[640,640]{1,0:T(8,128)(2,1)S(1)}, bf16[640,640]{1,0:T(8,128)(2,1)}, u32[]{:S(2)}) %copy-start.2) | copy-done | bytes 819224
  4.1 0.0 copy-start.3
  4.1 1.1 %copy-done.3 = bf16[640,640]{1,0:T(8,128)(2,1)S(1)} copy-done((bf16[640,640]{1,0:T(8,128)(2,1)S(1)}, bf16[640,640]{1,0:T(8,128)(2,1)}, u32[]{:S(2)}) %copy-start.3) | copy-done | bytes 819224
  5.2 0.0 copy-start.4
  5.2 1.1 %copy-done.4 = bf16[640,640]{1,0:T(8,128)(2,1)S(1)} copy-done((bf16[640,640]{1,0:T(8,128)(2,1)S(1)}, bf16[640,640]{1,0:T(8,128)(2,1)}, u32[]{:S(2)}) %copy-start.4) | copy-done | bytes 819224
  6.4 0.0 copy-start.5
  6.4 1.0 %copy-done.5 = bf16[1,1,256,640]{3,2,1,0:T(8,128)(2,1)S(1)} copy-done((bf16[1,1,256,640]{3,2,1,0:T(8,128)(2,1)S(1)}, bf16[1,1,256,640]{3,2,1,0:T(8,128)(2,1)}, u32[]{:S(2)}) %copy-start.5) | copy-done | bytes 327704
  7.3 0.0 copy-start.6
  7.3 0.7 %copy-done.6 = bf16[16,640]{1,0:T(8,128)(2,1)S(1)} copy-done((bf16[16,640]{1,0:T(8,128)(2,1)S(1)}, bf16[16,640]{1,0:T(8,128)(2,1)}, u32[]{:S(2)}) %copy-start.6) | copy-done | bytes 20504
  8.1 0.0 copy-start.7
  8.1 1.0 %copy-done.7 = f32[128,640]{1,0:T(8,128)S(1)} copy-done((f32[128,640]{1,0:T(8,128)S(1)}, f32[128,640]{1,0:T(8,128)}, u32[]{:S(2)}) %copy-start.7) | copy-done | bytes 327704
  9.0 40.6 %shard_map.122 = (bf16[32,8,640]{2,1,0:T(8,128)(2,1)S(1)}, bf16[32,8,640]{2,1,0:T(8,128)(2,1)S(1)}) custom-call(bf16[256,640]{1,0:T(8,128)(2,1)S(1)} %bitcast.5, bf16[16,640]{1,0:T(8,128)(2,1)S(1)} %copy-done.6, bf16[640,640]{1,0:T(8,128)(2,1)S(1)} %copy-done, bf16[640,640]{1,0:T(8,128)(2,1)S(1)} %copy-done.1, bf16[640,640]{1,0:T(8,128)(2,1)S(1)} %copy-done.2, ...), custom_call_target="tpu_custom_call" | custom-call | flops 3500000000 | bytes 8000000 | tf_op jit(solution)/shard_map/pallas_call | solution.py:274
  49.6 0.7 %copy.15 = bf16[1,1,256,640]{3,2,1,0:T(8,128)(2,1)} copy(bf16[1,1,256,640]{3,2,1,0:T(8,128)(2,1)S(1)} %bitcast.4) | data formatting | bytes 655360
  50.4 0.7 %copy.16 = bf16[1,1,256,640]{3,2,1,0:T(8,128)(2,1)} copy(bf16[1,1,256,640]{3,2,1,0:T(8,128)(2,1)S(1)} %bitcast.3) | data formatting | bytes 655360
Async XLA Ops:
  0.6 1.1 %copy-start = (bf16[640,640]{1,0:T(8,128)(2,1)S(1)}, bf16[640,640]{1,0:T(8,128)(2,1)}, u32[]{:S(2)}) copy-start(bf16[640,640]{1,0:T(8,128)(2,1)} %wq.1) | copy-start | bytes 2457604
  1.8 1.1 %copy-start.1 = (bf16[640,640]{1,0:T(8,128)(2,1)S(1)}, bf16[640,640]{1,0:T(8,128)(2,1)}, u32[]{:S(2)}) copy-start(bf16[640,640]{1,0:T(8,128)(2,1)} %wk.1) | copy-start | bytes 2457604
  2.9 1.1 %copy-start.2 = (bf16[640,640]{1,0:T(8,128)(2,1)S(1)}, bf16[640,640]{1,0:T(8,128)(2,1)}, u32[]{:S(2)}) copy-start(bf16[640,640]{1,0:T(8,128)(2,1)} %wv.1) | copy-start | bytes 2457604
  4.1 1.1 %copy-start.3 = (bf16[640,640]{1,0:T(8,128)(2,1)S(1)}, bf16[640,640]{1,0:T(8,128)(2,1)}, u32[]{:S(2)}) copy-start(bf16[640,640]{1,0:T(8,128)(2,1)} %wo.1) | copy-start | bytes 2457604
  5.2 1.1 %copy-start.4 = (bf16[640,640]{1,0:T(8,128)(2,1)S(1)}, bf16[640,640]{1,0:T(8,128)(2,1)}, u32[]{:S(2)}) copy-start(bf16[640,640]{1,0:T(8,128)(2,1)} %tq.1) | copy-start | bytes 2457604
  6.4 1.0 %copy-start.5 = (bf16[1,1,256,640]{3,2,1,0:T(8,128)(2,1)S(1)}, bf16[1,1,256,640]{3,2,1,0:T(8,128)(2,1)}, u32[]{:S(2)}) copy-start(bf16[1,1,256,640]{3,2,1,0:T(8,128)(2,1)} %param.11) | copy-start | bytes 983044
  7.3 0.7 %copy-start.6 = (bf16[16,640]{1,0:T(8,128)(2,1)S(1)}, bf16[16,640]{1,0:T(8,128)(2,1)}, u32[]{:S(2)}) copy-start(bf16[16,640]{1,0:T(8,128)(2,1)} %ref_hbm.1) | copy-start | bytes 61444
  8.1 1.0 %copy-start.7 = (f32[128,640]{1,0:T(8,128)S(1)}, f32[128,640]{1,0:T(8,128)}, u32[]{:S(2)}) copy-start(f32[128,640]{1,0:T(8,128)} %constant.2.clone.pe_hbm) | copy-start | bytes 983044

commit v2 on v1

--- a/solution.py
+++ b/solution.py
@@ -27,10 +27,11 @@
     [(a, b) for a in range(4) for b in range(4) if a or b],
     key=lambda o: -(2 * min(o[0], 4 - o[0]) + min(o[1], 4 - o[1])),
 )
-REF_PEERS = sorted(
-    [(a, b, c) for a in range(2) for b in range(4) for c in range(2) if a or b or c],
-    key=lambda o: -(2 * o[0] + 2 * min(o[1], 4 - o[1]) + o[2]),
-)
+REF_PEERS = sorted([(a, b) for a in range(2) for b in range(4) if a or b], key=lambda o: -(o[0] + min(o[1], 4 - o[1])))
+NEAR = [(0, 1), (0, 2), (0, 3), (1, 0), (3, 0)]
+ROW_PEERS = [(0, 1), (0, 2), (0, 3)]
+COLUMN_PEERS = [(1, 0), (3, 0)]
+HALF = TOKENS // 2
 
 
 def sinusoid(count, width):
@@ -75,6 +76,26 @@
     lane, inside = head_lanes(head)
     filler = jnp.where(lane == ones_lane(head), 1.0, 0.0)
     return jnp.where(inside, rows[:, start : start + wide], filler).astype(jnp.bfloat16)
+
+
+def part(queries, keys, values, head, above=None):
+    scores = lax.dot_general(queries, keys, (((1,), (1,)), ((), ())), preferred_element_type=jnp.float32)
+    top = jnp.max(scores, axis=-1, keepdims=True)
+    if above is not None:
+        top = jnp.maximum(top, above)
+    weights = jnp.exp2((scores - top) * FACTOR).astype(jnp.bfloat16)
+    return top, jnp.dot(weights, values, preferred_element_type=jnp.float32)
+
+
+def place(tiles, mixed, head):
+    start, wide, _ = slab(head)
+    _, inside = head_lanes(head)
+    for j in range(wide // 128):
+        tile, cut = start // 128 + j, slice(j * 128, (j + 1) * 128)
+        if tile in tiles:
+            tiles[tile] = jnp.where(inside[:, cut], mixed[:, cut], tiles[tile])
+        else:
+            tiles[tile] = mixed[:, cut]
 
 
 def attend(queries, keys_of, values_of, allowed=None):
@@ -91,13 +112,7 @@
         mixed = jnp.dot(weights, values_of(head), preferred_element_type=jnp.float32)
         at = ones_lane(head)
         mixed = mixed * (1.0 / mixed[:, at : at + 1])
-        lane, inside = head_lanes(head)
-        for j in range(wide // 128):
-            tile, cut = start // 128 + j, slice(j * 128, (j + 1) * 128)
-            if tile in tiles:
-                tiles[tile] = jnp.where(inside[:, cut], mixed[:, cut], tiles[tile])
-            else:
-                tiles[tile] = mixed[:, cut]
+        place(tiles, mixed, head)
     return jnp.concatenate([tiles[t] for t in range(WIDTH // 128)], axis=1)
 
 
@@ -108,18 +123,19 @@
 def kernel(
     lat_hbm, ref_hbm, wq, wk, wv, wo, tq, tk, tv, to, pe_hbm,
     out_s, out_v,
-    lat, ref_raw, ref_all, w, pe, queries, keys, values, own, got, back,
-    load_sem, ref_send, ref_recv, go_send, go_recv, back_send, back_recv, out_sem,
+    lat, ref_raw, ref_all, w, pe, queries, keys, mixed_own, top_own, own, got, back,
+    load_sem, ref_send, ref_recv, go_send, go_recv, back_send, back_recv, out_sem, row_sem, column_sem,
 ):
     mine_f, mine_r = lax.axis_index("frame"), lax.axis_index("ref")
     zh, y = mine_f // 4, mine_f % 4
-    zl, x, core = mine_r // 8, (mine_r // 2) % 4, mine_r % 2
+    place_r, core = mine_r // 2, mine_r % 2
+    zl, x = place_r // 4, place_r % 4
 
     def frame_at(offset):
         return ((zh + offset[0]) % 4) * 4 + (y + offset[1]) % 4
 
-    def ref_at(offset):
-        return (((zl + offset[0]) % 2) * 4 + (x + offset[1]) % 4) * 2 + (core + offset[2]) % 2
+    def place_at(offset):
+        return ((zl + offset[0]) % 2) * 4 + (x + offset[1]) % 4
 
     loads = [
         pltpu.make_async_copy(ref_hbm, ref_raw, load_sem.at[0]),
@@ -131,69 +147,94 @@
         for i, matrix in enumerate((wq, wk, wv, wo, tq, tk, tv, to))
     ]
     loads[0].start()
+    barrier = pltpu.get_barrier_semaphore()
+    sibling = (mine_f, place_r * 2 + 1 - core)
+    greeted = [(mine_f, place_at(offset) * 2 + core) for offset in REF_PEERS]
+    greeted += [sibling] + [(frame_at(offset), mine_r) for offset in NEAR]
+    for device in greeted:
+        pl.semaphore_signal(barrier, inc=1, device_id=device, device_id_type=MESH)
     loads[1].start()
     for copy in weights:
         copy.start()
     loads[2].start()
 
-    barrier = pltpu.get_barrier_semaphore()
-    for offset in FRAME_PEERS:
-        pl.semaphore_signal(barrier, inc=1, device_id=(frame_at(offset), mine_r), device_id_type=MESH)
-    for offset in REF_PEERS:
-        pl.semaphore_signal(barrier, inc=1, device_id=(mine_f, ref_at(offset)), device_id_type=MESH)
-
     loads[0].wait()
-    slot = pl.ds(pl.multiple_of(mine_r * PIECES, PIECES), PIECES)
+    slot = pl.ds(pl.multiple_of((core * 8 + place_r) * PIECES, PIECES), PIECES)
     ref_all[slot, :] = layer_norm(ref_raw[...].astype(jnp.float32)).astype(jnp.bfloat16)
-    pl.semaphore_wait(barrier, len(FRAME_PEERS) + len(REF_PEERS))
+    pl.semaphore_wait(barrier, len(greeted))
     ref_copies = []
     for k, offset in enumerate(REF_PEERS):
         copy = pltpu.make_async_remote_copy(
             src_ref=ref_all.at[slot, :], dst_ref=ref_all.at[slot, :],
-            send_sem=ref_send.at[k], recv_sem=ref_recv.at[mine_r],
-            device_id=(mine_f, ref_at(offset)), device_id_type=MESH,
+            send_sem=ref_send.at[k], recv_sem=ref_recv.at[place_r],
+            device_id=(mine_f, place_at(offset) * 2 + core), device_id_type=MESH,
         )
         copy.start()
         ref_copies.append(copy)
+    for offset in COLUMN_PEERS:
+        pl.semaphore_signal(column_sem, inc=1, device_id=(frame_at(offset), mine_r), device_id_type=MESH)
 
     loads[1].wait()
     normed = layer_norm(lat[...].astype(jnp.float32)).astype(jnp.bfloat16)
     weights[0].wait()
     queries[...] = project(normed, w[0]).astype(jnp.bfloat16)
     weights[1].wait()
-    keys[0:TOKENS, :] = project(normed, w[1]).astype(jnp.bfloat16)
+    keys[...] = project(normed, w[1]).astype(jnp.bfloat16)
     weights[2].wait()
     own_values = project(normed, w[2]).astype(jnp.bfloat16)
+
     for head in range(HEADS):
-        wide = slab(head)[1]
-        values[head, 0:TOKENS, 0:wide] = padded_values(own_values, head)
+        start, wide, _ = slab(head)
+        cut = slice(start, start + wide)
+        top, mixed = part(masked_queries(queries[...], head), keys[:, cut], padded_values(own_values, head), head)
+        mixed_own[head, :, 0:wide] = mixed
+        top_own[head] = jnp.broadcast_to(top, (TOKENS, 128))
+
+    pl.semaphore_wait(column_sem, len(COLUMN_PEERS))
+    for offset in ROW_PEERS:
+        pl.semaphore_signal(row_sem, inc=1, device_id=(frame_at(offset), mine_r), device_id_type=MESH)
 
     for k, offset in enumerate(REF_PEERS):
-        source = ref_at(offset)
-        there = pl.ds(pl.multiple_of(source * PIECES, PIECES), PIECES)
+        source = place_at(offset)
+        there = pl.ds(pl.multiple_of((core * 8 + source) * PIECES, PIECES), PIECES)
         pltpu.make_async_remote_copy(
             src_ref=ref_all.at[there, :], dst_ref=ref_all.at[there, :],
             send_sem=ref_send.at[k], recv_sem=ref_recv.at[source],
-            device_id=(mine_f, source), device_id_type=MESH,
+            device_id=(mine_f, source * 2 + core), device_id_type=MESH,
         ).wait_recv()
+    half = pl.ds(pl.multiple_of(core * HALF, HALF), HALF)
+    copy = pltpu.make_async_remote_copy(
+        src_ref=ref_all.at[half, :], dst_ref=ref_all.at[half, :],
+        send_sem=ref_send.at[8], recv_sem=ref_recv.at[8],
+        device_id=sibling, device_id_type=MESH,
+    )
+    copy.start()
+    ref_copies.append(copy)
+    weights[3].wait()
+    copy.wait_recv()
     reference = ref_all[...]
-    keys[TOKENS : 2 * TOKENS, :] = project(reference, w[1]).astype(jnp.bfloat16)
+    ref_keys = project(reference, w[1]).astype(jnp.bfloat16)
     ref_values = project(reference, w[2]).astype(jnp.bfloat16)
+
+    tiles = {}
     for head in range(HEADS):
-        wide = slab(head)[1]
-        values[head, TOKENS : 2 * TOKENS, 0:wide] = padded_values(ref_values, head)
-    weights[3].wait()
-
+        start, wide, _ = slab(head)
+        cut = slice(start, start + wide)
+        before = top_own[head]
+        top, mixed = part(
+            masked_queries(queries[...], head), ref_keys[:, cut], padded_values(ref_values, head), head, before[:, 0:1]
+        )
+        kept = jnp.exp2((before - top) * FACTOR)
+        mixed = mixed + mixed_own[head, :, 0:wide] * jnp.concatenate([kept] * (wide // 128), axis=1)
+        at = ones_lane(head)
+        place(tiles, mixed * (1.0 / mixed[:, at : at + 1]), head)
+    attended = jnp.concatenate([tiles[t] for t in range(WIDTH // 128)], axis=1).astype(jnp.bfloat16)
+    result = lat[...].astype(jnp.float32) + project(attended, w[3])
+    own[...] = result.reshape(CHUNKS, FRAMES, EACH, WIDTH).astype(jnp.bfloat16)
+
+    pl.semaphore_wait(row_sem, len(ROW_PEERS))
     go_copies, out_copies = [], []
     for chunk in range(CHUNKS):
-        rows = slice(chunk * ROWS, (chunk + 1) * ROWS)
-        attended = attend(
-            queries[rows, :],
-            lambda start, wide: keys[:, start : start + wide],
-            lambda head: values[head, :, 0 : slab(head)[1]],
-        ).astype(jnp.bfloat16)
-        result = lat[rows, :].astype(jnp.float32) + project(attended, w[3])
-        own[chunk] = result.reshape(FRAMES, EACH, WIDTH).astype(jnp.bfloat16)
         for k, offset in enumerate(FRAME_PEERS):
             target = frame_at(offset)
             copy = pltpu.make_async_remote_copy(
@@ -203,6 +244,7 @@
             )
             copy.start()
             go_copies.append(copy)
+    for chunk in range(CHUNKS):
         got[chunk, pl.ds(mine_f, 1)] = own[chunk, pl.ds(mine_f, 1)]
         copy = pltpu.make_async_copy(
             own.at[chunk], out_s.at[pl.ds(chunk * FRAMES, FRAMES)], out_sem.at[chunk]
@@ -267,6 +309,14 @@
         copy.wait()
 
 
+def hand_over(spatial, video, out_s, out_v, sem):
+    copies = [pltpu.make_async_copy(spatial, out_s, sem.at[0]), pltpu.make_async_copy(video, out_v, sem.at[1])]
+    for copy in copies:
+        copy.start()
+    for copy in copies:
+        copy.wait()
+
+
 def body(latents, ref_hidden, *matrices):
     any_space = pl.BlockSpec(memory_space=pl.ANY)
     pe = jnp.asarray(np.repeat(sinusoid(FRAMES, WIDTH), EACH, axis=0))
@@ -283,8 +333,9 @@
             pltpu.VMEM((8, WIDTH, WIDTH), jnp.bfloat16),
             pltpu.VMEM((ROWS, WIDTH), jnp.float32),
             pltpu.VMEM((TOKENS, WIDTH), jnp.bfloat16),
-            pltpu.VMEM((2 * TOKENS, WIDTH), jnp.bfloat16),
-            pltpu.VMEM((HEADS, 2 * TOKENS, 256), jnp.bfloat16),
+            pltpu.VMEM((TOKENS, WIDTH), jnp.bfloat16),
+            pltpu.VMEM((HEADS, TOKENS, 256), jnp.float32),
+            pltpu.VMEM((HEADS, TOKENS, 128), jnp.float32),
             pltpu.VMEM((CHUNKS, FRAMES, EACH, WIDTH), jnp.bfloat16),
             pltpu.VMEM((CHUNKS, FRAMES, EACH, WIDTH), jnp.bfloat16),
             pltpu.VMEM((CHUNKS, FRAMES, EACH, WIDTH), jnp.bfloat16),
@@ -296,12 +347,22 @@
             pltpu.SemaphoreType.DMA((CHUNKS, 16)),
             pltpu.SemaphoreType.DMA((CHUNKS, 16)),
             pltpu.SemaphoreType.DMA((2 * CHUNKS,)),
+            pltpu.SemaphoreType.REGULAR,
+            pltpu.SemaphoreType.REGULAR,
         ],
         compiler_params=pltpu.CompilerParams(
-            collective_id=0, has_side_effects=True, vmem_limit_bytes=48 * 2**20
+            collective_id=0, has_side_effects=True, vmem_limit_bytes=62 * 2**20
         ),
         cost_estimate=pl.CostEstimate(flops=3_500_000_000, bytes_accessed=8_000_000, transcendentals=1_500_000),
     )(latents.reshape(TOKENS, WIDTH), ref_hidden, *matrices, pe)
+    spatial, video = pl.pallas_call(
+        hand_over,
+        out_shape=(shape, shape),
+        in_specs=[any_space] * 2,
+        out_specs=(any_space, any_space),
+        scratch_shapes=[pltpu.SemaphoreType.DMA((2,))],
+        compiler_params=pltpu.CompilerParams(vmem_limit_bytes=62 * 2**20),
+    )(spatial, video)
     whole = (1, 1, TOKENS, WIDTH)
     return spatial.reshape(whole), video.reshape(whole)
 

time: 51.6 us -> 62.4 us (1.21)
  Pallas kernels: 40.6 us -> 61.6 us
  local copies, waits for them, and re-layouts: 9.84 us -> 0 us
    pallas_call x0 -> x1, Pallas kernels: none -> 21 us  [body(): pl.pallas_call(hand_over, out_shape=(shape, shape), in_specs=[any_space]...]
    unnamed x18 -> x0, local copies, waits for them, and re-layouts: 9.84 us -> none
where the time goes in v2:
time: 62.4 us; the launch traced here: 62.3 us
  Pallas kernels  61.6 us (99%)
  between operations  0.64 us (1%)
    pallas_call x1, Pallas kernels, body(): pl.pallas_call(kernel, out_shape=(shape, shape), in_specs=[any_space] * 1...  40.7 us
    pallas_call x1, Pallas kernels, body(): pl.pallas_call(hand_over, out_shape=(shape, shape), in_specs=[any_space]...  21 us

profile of v2, /device:TPU:1, one launch (start us, length us, event | category | flops | bytes accessed | tf_op | source)
XLA Modules:
  0.0 62.3 jit_solution(7883320787022743197)
XLA Ops:
  0.6 40.7 %shard_map.122 = (bf16[32,8,640]{2,1,0:T(8,128)(2,1)}, bf16[32,8,640]{2,1,0:T(8,128)(2,1)}) custom-call(bf16[256,640]{1,0:T(8,128)(2,1)} %bitcast.3, bf16[16,640]{1,0:T(8,128)(2,1)} %ref_hbm.1, bf16[640,640]{1,0:T(8,128)(2,1)} %wq.1, bf16[640,640]{1,0:T(8,128)(2,1)} %wk.1, bf16[640,640]{1,0:T(8,128)(2,1)} %wv.1, bf16[640,640]{1,0:T(8,128)(2,1)} %wo.1, ...), custom_call_target="tpu_custom_call" | custom-call | flops 3500000000 | bytes 8000000 | tf_op jit(solution)/shard_map/pallas_call | solution.py:324
  41.3 21.0 %shard_map.123 = (bf16[32,8,640]{2,1,0:T(8,128)(2,1)}, bf16[32,8,640]{2,1,0:T(8,128)(2,1)}) custom-call(bf16[32,8,640]{2,1,0:T(8,128)(2,1)} %get-tuple-element.6.spatial, bf16[32,8,640]{2,1,0:T(8,128)(2,1)} %get-tuple-element.7.video), custom_call_target="tpu_custom_call" | custom-call | tf_op jit(solution)/shard_map/pallas_call | solution.py:358

commit v3 on v2

--- a/solution.py
+++ b/solution.py
@@ -60,9 +60,8 @@
     return lane, (lane >= offset) & (lane < offset + DIM)
 
 
-def ones_lane(head):
-    start, wide, offset = slab(head)
-    return 0 if offset > 0 else wide - 1
+def sum_lane(head):
+    return head if head > 0 else 120
 
 
 def masked_queries(rows, head):
@@ -74,46 +73,48 @@
 def padded_values(rows, head):
     start, wide, _ = slab(head)
     lane, inside = head_lanes(head)
-    filler = jnp.where(lane == ones_lane(head), 1.0, 0.0)
+    filler = jnp.where(lane == sum_lane(head), 1.0, 0.0)
     return jnp.where(inside, rows[:, start : start + wide], filler).astype(jnp.bfloat16)
 
 
-def part(queries, keys, values, head, above=None):
-    scores = lax.dot_general(queries, keys, (((1,), (1,)), ((), ())), preferred_element_type=jnp.float32)
-    top = jnp.max(scores, axis=-1, keepdims=True)
-    if above is not None:
-        top = jnp.maximum(top, above)
-    weights = jnp.exp2((scores - top) * FACTOR).astype(jnp.bfloat16)
-    return top, jnp.dot(weights, values, preferred_element_type=jnp.float32)
-
-
-def place(tiles, mixed, head):
-    start, wide, _ = slab(head)
-    _, inside = head_lanes(head)
-    for j in range(wide // 128):
-        tile, cut = start // 128 + j, slice(j * 128, (j + 1) * 128)
-        if tile in tiles:
-            tiles[tile] = jnp.where(inside[:, cut], mixed[:, cut], tiles[tile])
-        else:
-            tiles[tile] = mixed[:, cut]
-
-
-def attend(queries, keys_of, values_of, allowed=None):
+def attend(queries, keys, values, allowed=None):
+    count = queries.shape[0]
+    lane = lax.broadcasted_iota(jnp.int32, (1, 128), 1)
+    tops, sums = jnp.zeros((count, 128), jnp.float32), jnp.ones((count, 128), jnp.float32)
     tiles = {}
     for head in range(HEADS):
-        start, wide, offset = slab(head)
+        start, wide, _ = slab(head)
+        _, inside = head_lanes(head)
         scores = lax.dot_general(
-            masked_queries(queries, head), keys_of(start, wide), (((1,), (1,)), ((), ())), preferred_element_type=jnp.float32
+            masked_queries(queries, head), keys[:, start : start + wide],
+            (((1,), (1,)), ((), ())), preferred_element_type=jnp.float32,
         )
         if allowed is not None:
             scores = jnp.where(allowed, scores, -1e30)
         top = jnp.max(scores, axis=-1, keepdims=True)
         weights = jnp.exp2((scores - top) * FACTOR).astype(jnp.bfloat16)
-        mixed = jnp.dot(weights, values_of(head), preferred_element_type=jnp.float32)
-        at = ones_lane(head)
-        mixed = mixed * (1.0 / mixed[:, at : at + 1])
-        place(tiles, mixed, head)
-    return jnp.concatenate([tiles[t] for t in range(WIDTH // 128)], axis=1)
+        mixed = jnp.dot(weights, padded_values(values, head), preferred_element_type=jnp.float32)
+        tops = jnp.where(lane == sum_lane(head), top, tops)
+        sums = jnp.where(lane == sum_lane(head), mixed[:, :128], sums)
+        for j in range(wide // 128):
+            tile, cut = start // 128 + j, slice(j * 128, (j + 1) * 128)
+            if tile in tiles:
+                tiles[tile] = jnp.where(inside[:, cut], mixed[:, cut], tiles[tile])
+            else:
+                tiles[tile] = mixed[:, cut]
+    return jnp.concatenate([tiles[t] for t in range(WIDTH // 128)], axis=1), tops, sums
+
+
+def head_columns():
+    lane = lax.broadcasted_iota(jnp.int32, (256, WIDTH), 0) % 128
+    head = lax.broadcasted_iota(jnp.int32, (256, WIDTH), 1) // DIM
+    return jnp.where(lane == jnp.where(head == 0, sum_lane(0), head), 1.0, 0.0).astype(jnp.bfloat16)
+
+
+def to_columns(factors, columns):
+    high = factors.astype(jnp.bfloat16)
+    low = (factors - high.astype(jnp.float32)).astype(jnp.bfloat16)
+    return project(jnp.concatenate([high, low], axis=1), columns)
 
 
 def project(rows, matrix):
@@ -123,7 +124,7 @@
 def kernel(
     lat_hbm, ref_hbm, wq, wk, wv, wo, tq, tk, tv, to, pe_hbm,
     out_s, out_v,
-    lat, ref_raw, ref_all, w, pe, queries, keys, mixed_own, top_own, own, got, back,
+    lat, ref_raw, ref_all, w, pe, queries, mixed_own, top_own, sum_own, columns, own, got, back,
     load_sem, ref_send, ref_recv, go_send, go_recv, back_send, back_recv, out_sem, row_sem, column_sem,
 ):
     mine_f, mine_r = lax.axis_index("frame"), lax.axis_index("ref")
@@ -179,16 +180,12 @@
     weights[0].wait()
     queries[...] = project(normed, w[0]).astype(jnp.bfloat16)
     weights[1].wait()
-    keys[...] = project(normed, w[1]).astype(jnp.bfloat16)
+    own_keys = project(normed, w[1]).astype(jnp.bfloat16)
     weights[2].wait()
     own_values = project(normed, w[2]).astype(jnp.bfloat16)
 
-    for head in range(HEADS):
-        start, wide, _ = slab(head)
-        cut = slice(start, start + wide)
-        top, mixed = part(masked_queries(queries[...], head), keys[:, cut], padded_values(own_values, head), head)
-        mixed_own[head, :, 0:wide] = mixed
-        top_own[head] = jnp.broadcast_to(top, (TOKENS, 128))
+    mixed_own[...], top_own[...], sum_own[...] = attend(queries[...], own_keys, own_values)
+    columns[...] = head_columns()
 
     pl.semaphore_wait(column_sem, len(COLUMN_PEERS))
     for offset in ROW_PEERS:
@@ -216,19 +213,12 @@
     ref_keys = project(reference, w[1]).astype(jnp.bfloat16)
     ref_values = project(reference, w[2]).astype(jnp.bfloat16)
 
-    tiles = {}
-    for head in range(HEADS):
-        start, wide, _ = slab(head)
-        cut = slice(start, start + wide)
-        before = top_own[head]
-        top, mixed = part(
-            masked_queries(queries[...], head), ref_keys[:, cut], padded_values(ref_values, head), head, before[:, 0:1]
-        )
-        kept = jnp.exp2((before - top) * FACTOR)
-        mixed = mixed + mixed_own[head, :, 0:wide] * jnp.concatenate([kept] * (wide // 128), axis=1)
-        at = ones_lane(head)
-        place(tiles, mixed * (1.0 / mixed[:, at : at + 1]), head)
-    attended = jnp.concatenate([tiles[t] for t in range(WIDTH // 128)], axis=1).astype(jnp.bfloat16)
+    mixed, top_ref, sum_ref = attend(queries[...], ref_keys, ref_values)
+    top = jnp.maximum(top_own[...], top_ref)
+    kept_own, kept_ref = jnp.exp2((top_own[...] - top) * FACTOR), jnp.exp2((top_ref - top) * FACTOR)
+    scale = 1.0 / (sum_own[...] * kept_own + sum_ref * kept_ref)
+    attended = mixed_own[...] * to_columns(kept_own * scale, columns[...])
+    attended = (attended + mixed * to_columns(kept_ref * scale, columns[...])).astype(jnp.bfloat16)
     result = lat[...].astype(jnp.float32) + project(attended, w[3])
     own[...] = result.reshape(CHUNKS, FRAMES, EACH, WIDTH).astype(jnp.bfloat16)
 
@@ -272,12 +262,8 @@
         time_queries = project(normed, w[4]).astype(jnp.bfloat16)
         time_keys = project(normed, w[5]).astype(jnp.bfloat16)
         time_values = project(normed, w[6]).astype(jnp.bfloat16)
-        attended = attend(
-            time_queries,
-            lambda start, wide: time_keys[:, start : start + wide],
-            lambda head: padded_values(time_values, head),
-            allowed,
-        ).astype(jnp.bfloat16)
+        mixed, _, total = attend(time_queries, time_keys, time_values, allowed)
+        attended = (mixed * to_columns(1.0 / total, columns[...])).astype(jnp.bfloat16)
         result = clip + project(attended, w[7])
         back[chunk] = result.reshape(FRAMES, EACH, WIDTH).astype(jnp.bfloat16)
         for k, offset in enumerate(FRAME_PEERS):
@@ -321,6 +307,7 @@
     any_space = pl.BlockSpec(memory_space=pl.ANY)
     pe = jnp.asarray(np.repeat(sinusoid(FRAMES, WIDTH), EACH, axis=0))
     shape = jax.ShapeDtypeStruct((CHUNKS * FRAMES, EACH, WIDTH), jnp.bfloat16)
+    operands = (latents.reshape(TOKENS, WIDTH), ref_hidden, *matrices, pe)
     spatial, video = pl.pallas_call(
         kernel,
         out_shape=(shape, shape),
@@ -333,9 +320,10 @@
             pltpu.VMEM((8, WIDTH, WIDTH), jnp.bfloat16),
             pltpu.VMEM((ROWS, WIDTH), jnp.float32),
             pltpu.VMEM((TOKENS, WIDTH), jnp.bfloat16),
-            pltpu.VMEM((TOKENS, WIDTH), jnp.bfloat16),
-            pltpu.VMEM((HEADS, TOKENS, 256), jnp.float32),
-            pltpu.VMEM((HEADS, TOKENS, 128), jnp.float32),
+            pltpu.VMEM((TOKENS, WIDTH), jnp.float32),
+            pltpu.VMEM((TOKENS, 128), jnp.float32),
+            pltpu.VMEM((TOKENS, 128), jnp.float32),
+            pltpu.VMEM((256, WIDTH), jnp.bfloat16),
             pltpu.VMEM((CHUNKS, FRAMES, EACH, WIDTH), jnp.bfloat16),
             pltpu.VMEM((CHUNKS, FRAMES, EACH, WIDTH), jnp.bfloat16),
             pltpu.VMEM((CHUNKS, FRAMES, EACH, WIDTH), jnp.bfloat16),
@@ -351,17 +339,17 @@
             pltpu.SemaphoreType.REGULAR,
         ],
         compiler_params=pltpu.CompilerParams(
-            collective_id=0, has_side_effects=True, vmem_limit_bytes=62 * 2**20
+            collective_id=0, has_side_effects=True, vmem_limit_bytes=48 * 2**20
         ),
         cost_estimate=pl.CostEstimate(flops=3_500_000_000, bytes_accessed=8_000_000, transcendentals=1_500_000),
-    )(latents.reshape(TOKENS, WIDTH), ref_hidden, *matrices, pe)
+    )(*[pltpu.with_memory_space_constraint(a, pltpu.HBM) for a in operands])
     spatial, video = pl.pallas_call(
         hand_over,
         out_shape=(shape, shape),
         in_specs=[any_space] * 2,
         out_specs=(any_space, any_space),
         scratch_shapes=[pltpu.SemaphoreType.DMA((2,))],
-        compiler_params=pltpu.CompilerParams(vmem_limit_bytes=62 * 2**20),
+        compiler_params=pltpu.CompilerParams(vmem_limit_bytes=48 * 2**20),
     )(spatial, video)
     whole = (1, 1, TOKENS, WIDTH)
     return spatial.reshape(whole), video.reshape(whole)

time: 62.4 us -> 40.1 us (0.64)
  Pallas kernels: 61.6 us -> 39.3 us
    pallas_call x1, Pallas kernels: 21 us -> 0.85 us  [body(): pl.pallas_call(hand_over, out_shape=(shape, shape), in_specs=[any_space]...]
    pallas_call x1, Pallas kernels: 40.7 us -> 38.5 us  [body(): pl.pallas_call(kernel, out_shape=(shape, shape), in_specs=[any_space] * 1...]
where the time goes in v3:
time: 40.1 us; the launch traced here: 40 us
  Pallas kernels  39.3 us (98%)
  between operations  0.64 us (2%)
    pallas_call x1, Pallas kernels, body(): pl.pallas_call(kernel, out_shape=(shape, shape), in_specs=[any_space] * 1...  38.5 us
    pallas_call x1, Pallas kernels, body(): pl.pallas_call(hand_over, out_shape=(shape, shape), in_specs=[any_space]...  0.85 us

profile of v3, /device:TPU:1, one launch (start us, length us, event | category | flops | bytes accessed | tf_op | source)
XLA Modules:
  0.0 40.0 jit_solution(10528207991856366905)
XLA Ops:
  0.6 38.5 %shard_map.122 = (bf16[32,8,640]{2,1,0:T(8,128)(2,1)S(1)}, bf16[32,8,640]{2,1,0:T(8,128)(2,1)S(1)}) custom-call(bf16[256,640]{1,0:T(8,128)(2,1)} %bitcast.3, bf16[16,640]{1,0:T(8,128)(2,1)} %ref_hbm.1, bf16[640,640]{1,0:T(8,128)(2,1)} %wq.1, bf16[640,640]{1,0:T(8,128)(2,1)} %wk.1, bf16[640,640]{1,0:T(8,128)(2,1)} %wv.1, bf16[640,640]{1,0:T(8,128)(2,1)} %wo.1, ...), custom_call_target="tpu_custom_call" | custom-call | flops 3500000000 | bytes 8000000 | tf_op jit(solution)/shard_map/pallas_call | solution.py:311
  39.1 0.9 %shard_map.123 = (bf16[32,8,640]{2,1,0:T(8,128)(2,1)}, bf16[32,8,640]{2,1,0:T(8,128)(2,1)}) custom-call(bf16[32,8,640]{2,1,0:T(8,128)(2,1)S(1)} %get-tuple-element.6.spatial, bf16[32,8,640]{2,1,0:T(8,128)(2,1)S(1)} %get-tuple-element.7.video), custom_call_target="tpu_custom_call" | custom-call | tf_op jit(solution)/shard_map/pallas_call | solution.py:346

commit v4 on v3

v4 whole, which is shorter than its diff:
```python
import functools
import math

import jax
import jax.numpy as jnp
import numpy as np
from jax import lax
from jax.experimental import pallas as pl
from jax.experimental.pallas import tpu as pltpu
from jax.sharding import PartitionSpec as P

MESH = pl.DeviceIdType.MESH
HEADS = 8
DIM = 80
WIDTH = 640
TOKENS = 256
FRAMES = 16
PIECES = 16
CHUNKS = 2
ROWS = TOKENS // CHUNKS
EACH = ROWS // FRAMES
EPSILON = 1e-05
SCALE = 1.0 / math.sqrt(DIM)
FACTOR = SCALE * math.log2(math.e)

FRAME_PEERS = sorted(
    [(a, b) for a in range(4) for b in range(4) if a or b],
    key=lambda o: -(2 * min(o[0], 4 - o[0]) + min(o[1], 4 - o[1])),
)
REF_PEERS = sorted([(a, b) for a in range(2) for b in range(4) if a or b], key=lambda o: -(o[0] + min(o[1], 4 - o[1])))
NEAR = [(0, 1), (0, 2), (0, 3), (1, 0), (3, 0)]
ROW_PEERS = [(0, 1), (0, 2), (0, 3)]
COLUMN_PEERS = [(1, 0), (3, 0)]
HALF = TOKENS // 2


def sinusoid(count, width):
    position = np.arange(count, dtype=np.float64)[:, None]
    pair = np.arange(width // 2, dtype=np.float64)[None, :]
    angle = position * np.exp(pair * (-2.0 * math.log(10000.0) / width))
    return np.stack([np.sin(angle), np.cos(angle)], axis=-1).reshape(count, width).astype(np.float32)


def layer_norm(rows):
    center = rows - jnp.mean(rows, axis=-1, keepdims=True)
    spread = jnp.mean(center * center, axis=-1, keepdims=True)
    return center * lax.rsqrt(spread + EPSILON)


GROUPS = (((0, 1, 2), 0), ((3,), 128), ((4,), 256), ((5, 6, 7), 384))


def sum_column(head):
    return 240 + head if head < 3 else {3: 128, 4: 256}.get(head, 384) + head


def attend(queries, keys, values, allowed=None):
    count = queries.shape[0]
    lane = lax.broadcasted_iota(jnp.int32, (1, 128), 1)
    column = lax.broadcasted_iota(jnp.int32, (1, 256), 1)
    tops, sums = jnp.zeros((count, 128), jnp.float32), jnp.ones((count, 128), jnp.float32)
    tiles = {}
    for heads, start in GROUPS:
        cut = slice(start, start + 256)
        stack = []
        for head in heads:
            inside = (column >= head * DIM - start) & (column < (head + 1) * DIM - start)
            stack.append(jnp.where(inside, queries[:, cut], 0.0).astype(jnp.bfloat16))
        scores = lax.dot_general(
            jnp.concatenate(stack, axis=0), keys[:, cut], (((1,), (1,)), ((), ())), preferred_element_type=jnp.float32
        )
        if allowed is not None:
            scores = jnp.where(jnp.concatenate([allowed] * len(heads), axis=0), scores, -1e30)
        top = jnp.max(scores, axis=-1, keepdims=True)
        weights = jnp.exp2((scores - top) * FACTOR).astype(jnp.bfloat16)
        window = values[:, cut]
        for head in heads:
            window = jnp.where(column == sum_column(head) - start, 1.0, window).astype(jnp.bfloat16)
        mixed = jnp.dot(weights, window, preferred_element_type=jnp.float32)
        for i, head in enumerate(heads):
            rows = slice(i * count, (i + 1) * count)
            here = lane == sum_column(head) % 128
            at = (sum_column(head) - start) // 128 * 128
            tops = jnp.where(here, top[rows], tops)
            sums = jnp.where(here, mixed[rows, at : at + 128], sums)
            for tile in range(head * DIM // 128, -(-(head + 1) * DIM // 128)):
                part = mixed[rows, tile * 128 - start : (tile + 1) * 128 - start]
                if tile in tiles:
                    inside = (lane >= head * DIM - tile * 128) & (lane < (head + 1) * DIM - tile * 128)
                    part = jnp.where(inside, part, tiles[tile])
                tiles[tile] = part
    return jnp.concatenate([tiles[t] for t in range(WIDTH // 128)], axis=1), tops, sums


def head_columns():
    lane = lax.broadcasted_iota(jnp.int32, (256, WIDTH), 0) % 128
    head = lax.broadcasted_iota(jnp.int32, (256, WIDTH), 1) // DIM
    return jnp.where(lane == jnp.where(head < 3, 112 + head, head), 1.0, 0.0).astype(jnp.bfloat16)


def to_columns(factors, columns):
    high = factors.astype(jnp.bfloat16)
    low = (factors - high.astype(jnp.float32)).astype(jnp.bfloat16)
    return project(jnp.concatenate([high, low], axis=1), columns)


def project(rows, matrix):
    return jnp.dot(rows, matrix, preferred_element_type=jnp.float32)


def kernel(
    lat_hbm, ref_hbm, wq, wk, wv, wo, tq, tk, tv, to, pe_hbm,
    out_s, out_v,
    lat, ref_raw, ref_all, w, pe, queries, mixed_own, top_own, sum_own, columns, flat, own, got, back,
    load_sem, ref_send, ref_recv, go_send, go_recv, back_send, back_recv, out_sem, row_sem, column_sem,
):
    mine_f, mine_r = lax.axis_index("frame"), lax.axis_index("ref")
    zh, y = mine_f // 4, mine_f % 4
    place_r, core = mine_r // 2, mine_r % 2
    zl, x = place_r // 4, place_r % 4

    def frame_at(offset):
        return ((zh + offset[0]) % 4) * 4 + (y + offset[1]) % 4

    def place_at(offset):
        return ((zl + offset[0]) % 2) * 4 + (x + offset[1]) % 4

    loads = [
        pltpu.make_async_copy(ref_hbm, ref_raw, load_sem.at[0]),
        pltpu.make_async_copy(lat_hbm, lat, load_sem.at[1]),
        pltpu.make_async_copy(pe_hbm, pe, load_sem.at[2]),
    ]
    weights = [
        pltpu.make_async_copy(matrix, w.at[i], load_sem.at[3 + i])
        for i, matrix in enumerate((wq, wk, wv, wo, tq, tk, tv, to))
    ]
    loads[0].start()
    barrier = pltpu.get_barrier_semaphore()
    sibling = (mine_f, place_r * 2 + 1 - core)
    greeted = [(mine_f, place_at(offset) * 2 + core) for offset in REF_PEERS]
    greeted += [sibling] + [(frame_at(offset), mine_r) for offset in NEAR]
    for device in greeted:
        pl.semaphore_signal(barrier, inc=1, device_id=device, device_id_type=MESH)
    loads[1].start()
    for copy in weights:
        copy.start()
    loads[2].start()

    loads[0].wait()
    slot = pl.ds(pl.multiple_of((core * 8 + place_r) * PIECES, PIECES), PIECES)
    ref_all[slot, :] = layer_norm(ref_raw[...].astype(jnp.float32)).astype(jnp.bfloat16)
    pl.semaphore_wait(barrier, len(greeted))
    for offset in REF_PEERS:
        copy = pltpu.make_async_remote_copy(
            src_ref=ref_all.at[slot, :], dst_ref=ref_all.at[slot, :],
            send_sem=ref_send.at[0], recv_sem=ref_recv.at[0],
            device_id=(mine_f, place_at(offset) * 2 + core), device_id_type=MESH,
        )
        copy.start()
    for offset in COLUMN_PEERS:
        pl.semaphore_signal(column_sem, inc=1, device_id=(frame_at(offset), mine_r), device_id_type=MESH)

    loads[1].wait()
    normed = layer_norm(lat[...].astype(jnp.float32)).astype(jnp.bfloat16)
    weights[0].wait()
    queries[...] = project(normed, w[0]).astype(jnp.bfloat16)
    weights[1].wait()
    own_keys = project(normed, w[1]).astype(jnp.bfloat16)
    weights[2].wait()
    own_values = project(normed, w[2]).astype(jnp.bfloat16)

    mixed_own[...], top_own[...], sum_own[...] = attend(queries[...], own_keys, own_values)
    columns[...] = head_columns()

    pl.semaphore_wait(column_sem, len(COLUMN_PEERS))
    for offset in ROW_PEERS:
        pl.semaphore_signal(row_sem, inc=1, device_id=(frame_at(offset), mine_r), device_id_type=MESH)

    first = pl.ds(0, len(REF_PEERS) * PIECES)
    from_peers = pltpu.make_async_remote_copy(
        src_ref=ref_all.at[first, :], dst_ref=ref_all.at[first, :],
        send_sem=ref_send.at[0], recv_sem=ref_recv.at[0], device_id=sibling, device_id_type=MESH,
    )
    from_peers.wait_recv()
    half = pl.ds(pl.multiple_of(core * HALF, HALF), HALF)
    to_sibling = pltpu.make_async_remote_copy(
        src_ref=ref_all.at[half, :], dst_ref=ref_all.at[half, :],
        send_sem=ref_send.at[1], recv_sem=ref_recv.at[1], device_id=sibling, device_id_type=MESH,
    )
    to_sibling.start()
    weights[3].wait()
    to_sibling.wait_recv()
    reference = ref_all[...]
    ref_keys = project(reference, w[1]).astype(jnp.bfloat16)
    ref_values = project(reference, w[2]).astype(jnp.bfloat16)

    mixed, top_ref, sum_ref = attend(queries[...], ref_keys, ref_values)
    top = jnp.maximum(top_own[...], top_ref)
    kept_own, kept_ref = jnp.exp2((top_own[...] - top) * FACTOR), jnp.exp2((top_ref - top) * FACTOR)
    scale = 1.0 / (sum_own[...] * kept_own + sum_ref * kept_ref)
    attended = mixed_own[...] * to_columns(kept_own * scale, columns[...])
    attended = (attended + mixed * to_columns(kept_ref * scale, columns[...])).astype(jnp.bfloat16)
    result = lat[...].astype(jnp.float32) + project(attended, w[3])
    own[...] = result.reshape(CHUNKS, FRAMES, EACH, WIDTH).astype(jnp.bfloat16)

    pl.semaphore_wait(row_sem, len(ROW_PEERS))
    for chunk in range(CHUNKS):
        for offset in FRAME_PEERS:
            target = frame_at(offset)
            pltpu.make_async_remote_copy(
                src_ref=own.at[chunk, target], dst_ref=got.at[chunk, mine_f],
                send_sem=go_send.at[chunk], recv_sem=go_recv.at[chunk],
                device_id=(target, mine_r), device_id_type=MESH,
            ).start()
    out_copies = []
    for chunk in range(CHUNKS):
        got[chunk, pl.ds(mine_f, 1)] = own[chunk, pl.ds(mine_f, 1)]
    flat[...] = result.astype(jnp.bfloat16)
    copy = pltpu.make_async_copy(flat, out_s, out_sem.at[CHUNKS])
    copy.start()
    out_copies.append(copy)

    loads[2].wait()
    for copy in weights[4:]:
        copy.wait()
    from_peers.wait_send()
    to_sibling.wait_send()
    row = lax.broadcasted_iota(jnp.int32, (ROWS, ROWS), 0)
    column = lax.broadcasted_iota(jnp.int32, (ROWS, ROWS), 1)
    allowed = row % EACH == column % EACH
    others = pl.ds(0, len(FRAME_PEERS))
    for chunk in range(CHUNKS):
        whole = pltpu.make_async_remote_copy(
            src_ref=own.at[chunk, others], dst_ref=got.at[chunk, others],
            send_sem=go_send.at[chunk], recv_sem=go_recv.at[chunk], device_id=sibling, device_id_type=MESH,
        )
        whole.wait_recv()
        clip = got[chunk].astype(jnp.float32).reshape(ROWS, WIDTH)
        normed = (layer_norm(clip) + pe[...]).astype(jnp.bfloat16)
        time_queries = project(normed, w[4]).astype(jnp.bfloat16)
        time_keys = project(normed, w[5]).astype(jnp.bfloat16)
        time_values = project(normed, w[6]).astype(jnp.bfloat16)
        mixed, _, total = attend(time_queries, time_keys, time_values, allowed)
        attended = (mixed * to_columns(1.0 / total, columns[...])).astype(jnp.bfloat16)
        result = clip + project(attended, w[7])
        back[chunk] = result.reshape(FRAMES, EACH, WIDTH).astype(jnp.bfloat16)
        for offset in FRAME_PEERS:
            target = frame_at(offset)
            pltpu.make_async_remote_copy(
                src_ref=back.at[chunk, target], dst_ref=out_v.at[chunk * FRAMES + mine_f],
                send_sem=back_send.at[chunk], recv_sem=back_recv.at[chunk],
                device_id=(target, mine_r), device_id_type=MESH,
            ).start()
        copy = pltpu.make_async_copy(
            back.at[chunk, mine_f], out_v.at[chunk * FRAMES + mine_f], out_sem.at[chunk]
        )
        copy.start()
        out_copies.append(copy)
        whole.wait_send()

    for copy in out_copies:
        copy.wait()
    for chunk in range(CHUNKS):
        whole = pltpu.make_async_remote_copy(
            src_ref=back.at[chunk, others], dst_ref=out_v.at[pl.ds(chunk * FRAMES, len(FRAME_PEERS))],
            send_sem=back_send.at[chunk], recv_sem=back_recv.at[chunk], device_id=sibling, device_id_type=MESH,
        )
        whole.wait_send()
        whole.wait_recv()


def hand_over(spatial, video, out_s, out_v, held, sem):
    copies = [pltpu.make_async_copy(spatial, out_s, sem.at[0]), pltpu.make_async_copy(held, out_v, sem.at[1])]
    copies[0].start()
    held[...] = video[...].astype(jnp.float32).reshape(TOKENS, WIDTH).astype(jnp.bfloat16)
    copies[1].start()
    for copy in copies:
        copy.wait()


def body(latents, ref_hidden, *matrices):
    any_space = pl.BlockSpec(memory_space=pl.ANY)
    pe = jnp.asarray(np.repeat(sinusoid(FRAMES, WIDTH), EACH, axis=0))
    shape = jax.ShapeDtypeStruct((TOKENS, WIDTH), jnp.bfloat16)
    pieces = jax.ShapeDtypeStruct((CHUNKS * FRAMES, EACH, WIDTH), jnp.bfloat16)
    operands = (latents.reshape(TOKENS, WIDTH), ref_hidden, *matrices, pe)
    spatial, video = pl.pallas_call(
        kernel,
        out_shape=(shape, pieces),
        in_specs=[any_space] * 11,
        out_specs=(any_space, any_space),
        scratch_shapes=[
            pltpu.VMEM((TOKENS, WIDTH), jnp.bfloat16),
            pltpu.VMEM((PIECES, WIDTH), jnp.bfloat16),
            pltpu.VMEM((TOKENS, WIDTH), jnp.bfloat16),
            pltpu.VMEM((8, WIDTH, WIDTH), jnp.bfloat16),
            pltpu.VMEM((ROWS, WIDTH), jnp.float32),
            pltpu.VMEM((TOKENS, WIDTH), jnp.bfloat16),
            pltpu.VMEM((TOKENS, WIDTH), jnp.float32),
            pltpu.VMEM((TOKENS, 128), jnp.float32),
            pltpu.VMEM((TOKENS, 128), jnp.float32),
            pltpu.VMEM((256, WIDTH), jnp.bfloat16),
            pltpu.VMEM((TOKENS, WIDTH), jnp.bfloat16),
            pltpu.VMEM((CHUNKS, FRAMES, EACH, WIDTH), jnp.bfloat16),
            pltpu.VMEM((CHUNKS, FRAMES, EACH, WIDTH), jnp.bfloat16),
            pltpu.VMEM((CHUNKS, FRAMES, EACH, WIDTH), jnp.bfloat16),
            pltpu.SemaphoreType.DMA((11,)),
            pltpu.SemaphoreType.DMA((2,)),
            pltpu.SemaphoreType.DMA((2,)),
            pltpu.SemaphoreType.DMA((CHUNKS,)),
            pltpu.SemaphoreType.DMA((CHUNKS,)),
            pltpu.SemaphoreType.DMA((CHUNKS,)),
            pltpu.SemaphoreType.DMA((CHUNKS,)),
            pltpu.SemaphoreType.DMA((CHUNKS + 1,)),
            pltpu.SemaphoreType.REGULAR,
            pltpu.SemaphoreType.REGULAR,
        ],
        compiler_params=pltpu.CompilerParams(
            collective_id=0, has_side_effects=True, vmem_limit_bytes=48 * 2**20
        ),
        cost_estimate=pl.CostEstimate(flops=3_500_000_000, bytes_accessed=8_000_000, transcendentals=1_500_000),
    )(*[pltpu.with_memory_space_constraint(a, pltpu.HBM) for a in operands])
    spatial, video = pl.pallas_call(
        hand_over,
        out_shape=(shape, shape),
        in_specs=[any_space, pl.BlockSpec(memory_space=pltpu.VMEM)],
        out_specs=(any_space, any_space),
        scratch_shapes=[pltpu.VMEM((TOKENS, WIDTH), jnp.bfloat16), pltpu.SemaphoreType.DMA((2,))],
        compiler_params=pltpu.CompilerParams(vmem_limit_bytes=48 * 2**20),
    )(spatial, video)
    whole = (1, 1, TOKENS, WIDTH)
    return spatial.reshape(whole), video.reshape(whole)


def solution(mesh):
    split = P("ref", "frame", None, None)
    return jax.shard_map(
        body,
        mesh=mesh,
        in_specs=(split, P("ref", None)) + (P(),) * 8,
        out_specs=(split, split),
        check_vma=False,
    )
```

time: 40.1 us -> 37.5 us (0.935)
  Pallas kernels: 39.3 us -> 36.8 us
    pallas_call x2, Pallas kernels: 39.3 us -> 36.8 us  [the longest x1 35.9 us: body(): pl.pallas_call(kernel, out_shape=(shape, pieces), in_specs=[any_space] *...]
where the time goes in v4:
time: 37.5 us; the launch traced here: 37.4 us
  Pallas kernels  36.8 us (98%)
  between operations  0.64 us (2%)
    pallas_call x1, Pallas kernels, body(): pl.pallas_call(kernel, out_shape=(shape, pieces), in_specs=[any_space] *...  35.9 us
    pallas_call x1, Pallas kernels, body(): pl.pallas_call(hand_over, out_shape=(shape, shape), in_specs=[any_space,...  0.85 us

profile of v4, /device:TPU:1, one launch (start us, length us, event | category | flops | bytes accessed | tf_op | source)
XLA Modules:
  0.0 37.4 jit_solution(15227659481928467918)
XLA Ops:
  0.6 35.9 %shard_map.122 = (bf16[256,640]{1,0:T(8,128)(2,1)S(1)}, bf16[32,8,640]{2,1,0:T(8,128)(2,1)S(1)}) custom-call(bf16[256,640]{1,0:T(8,128)(2,1)} %bitcast.3, bf16[16,640]{1,0:T(8,128)(2,1)} %ref_hbm.1, bf16[640,640]{1,0:T(8,128)(2,1)} %wq.1, bf16[640,640]{1,0:T(8,128)(2,1)} %wk.1, bf16[640,640]{1,0:T(8,128)(2,1)} %wv.1, bf16[640,640]{1,0:T(8,128)(2,1)} %wo.1, ...), custom_call_target="tpu_custom_call" | custom-call | flops 3500000000 | bytes 8000000 | tf_op jit(solution)/shard_map/pallas_call | solution.py:287
  36.5 0.9 %shard_map.123 = (bf16[256,640]{1,0:T(8,128)(2,1)}, bf16[256,640]{1,0:T(8,128)(2,1)}) custom-call(bf16[256,640]{1,0:T(8,128)(2,1)S(1)} %get-tuple-element.6.spatial, bf16[32,8,640]{2,1,0:T(8,128)(2,1)S(1)} %get-tuple-element.7.video), custom_call_target="tpu_custom_call" | custom-call | tf_op jit(solution)/shard_map/pallas_call | solution.py:323

commit v5 on v4

--- a/solution.py
+++ b/solution.py
@@ -194,28 +194,31 @@
     ref_keys = project(reference, w[1]).astype(jnp.bfloat16)
     ref_values = project(reference, w[2]).astype(jnp.bfloat16)
 
-    mixed, top_ref, sum_ref = attend(queries[...], ref_keys, ref_values)
-    top = jnp.maximum(top_own[...], top_ref)
-    kept_own, kept_ref = jnp.exp2((top_own[...] - top) * FACTOR), jnp.exp2((top_ref - top) * FACTOR)
-    scale = 1.0 / (sum_own[...] * kept_own + sum_ref * kept_ref)
-    attended = mixed_own[...] * to_columns(kept_own * scale, columns[...])
-    attended = (attended + mixed * to_columns(kept_ref * scale, columns[...])).astype(jnp.bfloat16)
-    result = lat[...].astype(jnp.float32) + project(attended, w[3])
-    own[...] = result.reshape(CHUNKS, FRAMES, EACH, WIDTH).astype(jnp.bfloat16)
-
-    pl.semaphore_wait(row_sem, len(ROW_PEERS))
-    for chunk in range(CHUNKS):
-        for offset in FRAME_PEERS:
-            target = frame_at(offset)
-            pltpu.make_async_remote_copy(
-                src_ref=own.at[chunk, target], dst_ref=got.at[chunk, mine_f],
-                send_sem=go_send.at[chunk], recv_sem=go_recv.at[chunk],
-                device_id=(target, mine_r), device_id_type=MESH,
-            ).start()
+    for part in range(2):
+        rows = slice(part * HALF, (part + 1) * HALF)
+        mixed, top_ref, sum_ref = attend(queries[rows, :], ref_keys, ref_values)
+        top = jnp.maximum(top_own[rows, :], top_ref)
+        kept_own, kept_ref = jnp.exp2((top_own[rows, :] - top) * FACTOR), jnp.exp2((top_ref - top) * FACTOR)
+        scale = 1.0 / (sum_own[rows, :] * kept_own + sum_ref * kept_ref)
+        attended = mixed_own[rows, :] * to_columns(kept_own * scale, columns[...])
+        attended = (attended + mixed * to_columns(kept_ref * scale, columns[...])).astype(jnp.bfloat16)
+        result = lat[rows, :].astype(jnp.float32) + project(attended, w[3])
+        chunks = slice(part * CHUNKS // 2, (part + 1) * CHUNKS // 2)
+        own[chunks] = result.reshape(CHUNKS // 2, FRAMES, EACH, WIDTH).astype(jnp.bfloat16)
+        flat[rows, :] = result.astype(jnp.bfloat16)
+        if part == 0:
+            pl.semaphore_wait(row_sem, len(ROW_PEERS))
+        for chunk in range(CHUNKS)[chunks]:
+            for offset in FRAME_PEERS:
+                target = frame_at(offset)
+                pltpu.make_async_remote_copy(
+                    src_ref=own.at[chunk, target], dst_ref=got.at[chunk, mine_f],
+                    send_sem=go_send.at[chunk], recv_sem=go_recv.at[chunk],
+                    device_id=(target, mine_r), device_id_type=MESH,
+                ).start()
     out_copies = []
     for chunk in range(CHUNKS):
         got[chunk, pl.ds(mine_f, 1)] = own[chunk, pl.ds(mine_f, 1)]
-    flat[...] = result.astype(jnp.bfloat16)
     copy = pltpu.make_async_copy(flat, out_s, out_sem.at[CHUNKS])
     copy.start()
     out_copies.append(copy)
@@ -244,13 +247,15 @@
         attended = (mixed * to_columns(1.0 / total, columns[...])).astype(jnp.bfloat16)
         result = clip + project(attended, w[7])
         back[chunk] = result.reshape(FRAMES, EACH, WIDTH).astype(jnp.bfloat16)
-        for offset in FRAME_PEERS:
-            target = frame_at(offset)
+        def send_back(target, chunk=chunk):
             pltpu.make_async_remote_copy(
                 src_ref=back.at[chunk, target], dst_ref=out_v.at[chunk * FRAMES + mine_f],
                 send_sem=back_send.at[chunk], recv_sem=back_recv.at[chunk],
                 device_id=(target, mine_r), device_id_type=MESH,
             ).start()
+
+        pl.loop(0, mine_f)(send_back)
+        pl.loop(mine_f + 1, FRAMES)(send_back)
         copy = pltpu.make_async_copy(
             back.at[chunk, mine_f], out_v.at[chunk * FRAMES + mine_f], out_sem.at[chunk]
         )

time: 37.5 us -> 36.4 us (0.971)
  Pallas kernels: 36.8 us -> 35.7 us
    pallas_call x1, Pallas kernels: 35.9 us -> 34.9 us  [body(): pl.pallas_call(kernel, out_shape=(shape, pieces), in_specs=[any_space] *...]
where the time goes in v5:
time: 36.4 us
  Pallas kernels  35.7 us (98%)
  between operations  0.64 us (2%)
    pallas_call x1, Pallas kernels, body(): pl.pallas_call(kernel, out_shape=(shape, pieces), in_specs=[any_space] *...  34.9 us
    pallas_call x1, Pallas kernels, body(): pl.pallas_call(hand_over, out_shape=(shape, shape), in_specs=[any_space,...  0.85 us

profile of v5, /device:TPU:1, one launch (start us, length us, event | category | flops | bytes accessed | tf_op | source)
XLA Modules:
  0.0 36.4 jit_solution(14405205448043425497)
XLA Ops:
  0.6 34.9 %shard_map.122 = (bf16[256,640]{1,0:T(8,128)(2,1)S(1)}, bf16[32,8,640]{2,1,0:T(8,128)(2,1)S(1)}) custom-call(bf16[256,640]{1,0:T(8,128)(2,1)} %bitcast.3, bf16[16,640]{1,0:T(8,128)(2,1)} %ref_hbm.1, bf16[640,640]{1,0:T(8,128)(2,1)} %wq.1, bf16[640,640]{1,0:T(8,128)(2,1)} %wk.1, bf16[640,640]{1,0:T(8,128)(2,1)} %wv.1, bf16[640,640]{1,0:T(8,128)(2,1)} %wo.1, ...), custom_call_target="tpu_custom_call" | custom-call | flops 3500000000 | bytes 8000000 | tf_op jit(solution)/shard_map/pallas_call | solution.py:292
  35.5 0.9 %shard_map.123 = (bf16[256,640]{1,0:T(8,128)(2,1)}, bf16[256,640]{1,0:T(8,128)(2,1)}) custom-call(bf16[256,640]{1,0:T(8,128)(2,1)S(1)} %get-tuple-element.6.spatial, bf16[32,8,640]{2,1,0:T(8,128)(2,1)S(1)} %get-tuple-element.7.video), custom_call_target="tpu_custom_call" | custom-call | tf_op jit(solution)/shard_map/pallas_call | solution.py:328

commit v6 on v5

--- a/solution.py
+++ b/solution.py
@@ -131,7 +131,7 @@
         pltpu.make_async_copy(pe_hbm, pe, load_sem.at[2]),
     ]
     weights = [
-        pltpu.make_async_copy(matrix, w.at[i], load_sem.at[3 + i])
+        pltpu.make_async_copy(matrix, w.at[:, pl.ds(i * WIDTH, WIDTH)], load_sem.at[3 + i])
         for i, matrix in enumerate((wq, wk, wv, wo, tq, tk, tv, to))
     ]
     loads[0].start()
@@ -163,11 +163,11 @@
     loads[1].wait()
     normed = layer_norm(lat[...].astype(jnp.float32)).astype(jnp.bfloat16)
     weights[0].wait()
-    queries[...] = project(normed, w[0]).astype(jnp.bfloat16)
+    queries[...] = project(normed, w[:, 0 * WIDTH : 1 * WIDTH]).astype(jnp.bfloat16)
     weights[1].wait()
-    own_keys = project(normed, w[1]).astype(jnp.bfloat16)
+    own_keys = project(normed, w[:, 1 * WIDTH : 2 * WIDTH]).astype(jnp.bfloat16)
     weights[2].wait()
-    own_values = project(normed, w[2]).astype(jnp.bfloat16)
+    own_values = project(normed, w[:, 2 * WIDTH : 3 * WIDTH]).astype(jnp.bfloat16)
 
     mixed_own[...], top_own[...], sum_own[...] = attend(queries[...], own_keys, own_values)
     columns[...] = head_columns()
@@ -191,8 +191,8 @@
     weights[3].wait()
     to_sibling.wait_recv()
     reference = ref_all[...]
-    ref_keys = project(reference, w[1]).astype(jnp.bfloat16)
-    ref_values = project(reference, w[2]).astype(jnp.bfloat16)
+    both = project(reference, w[:, WIDTH : 3 * WIDTH]).astype(jnp.bfloat16)
+    ref_keys, ref_values = both[:, :WIDTH], both[:, WIDTH:]
 
     for part in range(2):
         rows = slice(part * HALF, (part + 1) * HALF)
@@ -202,7 +202,7 @@
         scale = 1.0 / (sum_own[rows, :] * kept_own + sum_ref * kept_ref)
         attended = mixed_own[rows, :] * to_columns(kept_own * scale, columns[...])
         attended = (attended + mixed * to_columns(kept_ref * scale, columns[...])).astype(jnp.bfloat16)
-        result = lat[rows, :].astype(jnp.float32) + project(attended, w[3])
+        result = lat[rows, :].astype(jnp.float32) + project(attended, w[:, 3 * WIDTH : 4 * WIDTH])
         chunks = slice(part * CHUNKS // 2, (part + 1) * CHUNKS // 2)
         own[chunks] = result.reshape(CHUNKS // 2, FRAMES, EACH, WIDTH).astype(jnp.bfloat16)
         flat[rows, :] = result.astype(jnp.bfloat16)
@@ -240,12 +240,11 @@
         whole.wait_recv()
         clip = got[chunk].astype(jnp.float32).reshape(ROWS, WIDTH)
         normed = (layer_norm(clip) + pe[...]).astype(jnp.bfloat16)
-        time_queries = project(normed, w[4]).astype(jnp.bfloat16)
-        time_keys = project(normed, w[5]).astype(jnp.bfloat16)
-        time_values = project(normed, w[6]).astype(jnp.bfloat16)
+        rows = project(normed, w[:, 4 * WIDTH : 7 * WIDTH]).astype(jnp.bfloat16)
+        time_queries, time_keys, time_values = (rows[:, i * WIDTH : (i + 1) * WIDTH] for i in range(3))
         mixed, _, total = attend(time_queries, time_keys, time_values, allowed)
         attended = (mixed * to_columns(1.0 / total, columns[...])).astype(jnp.bfloat16)
-        result = clip + project(attended, w[7])
+        result = clip + project(attended, w[:, 7 * WIDTH : 8 * WIDTH])
         back[chunk] = result.reshape(FRAMES, EACH, WIDTH).astype(jnp.bfloat16)
         def send_back(target, chunk=chunk):
             pltpu.make_async_remote_copy(
@@ -298,7 +297,7 @@
             pltpu.VMEM((TOKENS, WIDTH), jnp.bfloat16),
             pltpu.VMEM((PIECES, WIDTH), jnp.bfloat16),
             pltpu.VMEM((TOKENS, WIDTH), jnp.bfloat16),
-            pltpu.VMEM((8, WIDTH, WIDTH), jnp.bfloat16),
+            pltpu.VMEM((WIDTH, 8 * WIDTH), jnp.bfloat16),
             pltpu.VMEM((ROWS, WIDTH), jnp.float32),
             pltpu.VMEM((TOKENS, WIDTH), jnp.bfloat16),
             pltpu.VMEM((TOKENS, WIDTH), jnp.float32),

time: 36.4 us -> 36.6 us (level)
  no operation moved by 1% of the time
where the time goes in v6:
time: 36.6 us; the launch traced here: 36.5 us
  Pallas kernels  35.8 us (98%)
  between operations  0.64 us (2%)
    pallas_call x1, Pallas kernels, body(): pl.pallas_call(kernel, out_shape=(shape, pieces), in_specs=[any_space] *...  35 us
    pallas_call x1, Pallas kernels, body(): pl.pallas_call(hand_over, out_shape=(shape, shape), in_specs=[any_space,...  0.85 us

profile of v6, /device:TPU:1, one launch (start us, length us, event | category | flops | bytes accessed | tf_op | source)
XLA Modules:
  0.0 36.5 jit_solution(8887662175939804119)
XLA Ops:
  0.6 35.0 %shard_map.122 = (bf16[256,640]{1,0:T(8,128)(2,1)S(1)}, bf16[32,8,640]{2,1,0:T(8,128)(2,1)S(1)}) custom-call(bf16[256,640]{1,0:T(8,128)(2,1)} %bitcast.3, bf16[16,640]{1,0:T(8,128)(2,1)} %ref_hbm.1, bf16[640,640]{1,0:T(8,128)(2,1)} %wq.1, bf16[640,640]{1,0:T(8,128)(2,1)} %wk.1, bf16[640,640]{1,0:T(8,128)(2,1)} %wv.1, bf16[640,640]{1,0:T(8,128)(2,1)} %wo.1, ...), custom_call_target="tpu_custom_call" | custom-call | flops 3500000000 | bytes 8000000 | tf_op jit(solution)/shard_map/pallas_call | solution.py:291
  35.6 0.9 %shard_map.123 = (bf16[256,640]{1,0:T(8,128)(2,1)}, bf16[256,640]{1,0:T(8,128)(2,1)}) custom-call(bf16[256,640]{1,0:T(8,128)(2,1)S(1)} %get-tuple-element.6.spatial, bf16[32,8,640]{2,1,0:T(8,128)(2,1)S(1)} %get-tuple-element.7.video), custom_call_target="tpu_custom_call" | custom-call | tf_op jit(solution)/shard_map/pallas_call | solution.py:327
